TPU v7x, 32 devices: a whole 2x2x4 slice. The times are simulated.
32 devices in a mesh: section: 2 (over y), sx: 8 (over z, core), sy: 2 (over x).
Axes of the slice: x: 2, y: 2, z: 4, core: 2. Of those that a mesh axis runs over, the one named last changes fastest.
Arguments:
- previous: float32 [16, 128, 256], P(None, 'sx', 'sy'), may hold values from -3 to 3
- sections: float32 [4, 16, 128, 256], P('section', None, 'sx', 'sy'), may hold values from -3 to 3
- diffusivity: float32 [16, 128, 256], P(None, 'sx', 'sy'), may hold values from 0.3 to 3
- reaction: float32 [16, 128, 256], P(None, 'sx', 'sy'), may hold values from 0.2 to 2
Outputs:
- updated: float32 [4, 16, 128, 256], P('section', None, 'sx', 'sy')
All inputs are finite; a program needn't handle non-finite values.
Results may differ from a plain program's by a relative error of at most 0.0003.
Values sent between devices are 32-bit elements; how exact they have to be, the bound alone decides.
A program may use at most 64 MiB of HBM per device.

v0:
```python
import jax
import jax.numpy as jnp
from jax import lax
from jax.sharding import PartitionSpec as P

ITERS = 4


step_size = 1.0
tiny_value = 1e-06


def extended(cells, sides, width):
    for axis, dim in sides:
        count = lax.axis_size(axis)
        ends = count - 1
        head = lax.slice_in_dim(cells, 0, width, axis=dim)
        tail = lax.slice_in_dim(cells, cells.shape[dim] - width, cells.shape[dim], axis=dim)
        cells = jnp.concatenate(
            [
                lax.ppermute(tail, axis, [(i, (i + 1) % count) for i in range(ends)]),
                cells,
                lax.ppermute(head, axis, [((i + 1) % count, i) for i in range(ends)]),
            ],
            axis=dim,
        )
    return cells


def invert_table(matrix):
    order_n = len(matrix)
    augmented = [
        list(matrix[r]) + [1.0 if c == r else 0.0 for c in range(order_n)] for r in range(order_n)
    ]
    for col in range(order_n):
        pivot_row = max(range(col, order_n), key=lambda r: abs(augmented[r][col]))
        augmented[col], augmented[pivot_row] = (augmented[pivot_row], augmented[col])
        leading = augmented[col][col]
        augmented[col] = [v / leading for v in augmented[col]]
        for r in range(order_n):
            if r != col:
                factor = augmented[r][col]
                augmented[r] = [a - factor * b for a, b in zip(augmented[r], augmented[col])]
    return [row_values[order_n:] for row_values in augmented]


def table_product(left, right):
    return [
        [sum((left[i][k] * right[k][j] for k in range(len(right)))) for j in range(len(right[0]))]
        for i in range(len(left))
    ]


def pair_add(first, second):
    return (first[0] + second[0], first[1] + second[1])


def pair_sub(first, second):
    return (first[0] - second[0], first[1] - second[1])


def pair_mul(first, second):
    return (
        first[0] * second[0] - first[1] * second[1],
        first[0] * second[1] + first[1] * second[0],
    )


def pair_div(first, second):
    scale_sq = second[0] * second[0] + second[1] * second[1]
    return (
        (first[0] * second[0] + first[1] * second[1]) / scale_sq,
        (first[1] * second[0] - first[0] * second[1]) / scale_sq,
    )


def quartic_value(point):
    return (((210.0 * point - 480.0) * point + 360.0) * point - 96.0) * point + 6.0


def bisect_root(lower, upper):
    for count in range(200):
        middle = 0.5 * (lower + upper)
        if (quartic_value(lower) < 0.0) == (quartic_value(middle) < 0.0):
            lower = middle
        else:
            upper = middle
    return 0.5 * (lower + upper)


def radau_tables():
    abscissae = []
    grid_steps = 4000
    for m in range(grid_steps):
        lower = 0.999 * m / grid_steps
        upper = 0.999 * (m + 1) / grid_steps
        if (quartic_value(lower) < 0.0) != (quartic_value(upper) < 0.0):
            abscissae.append(bisect_root(lower, upper))
    abscissae.append(1.0)
    vander = [[abscissae[j] ** k for k in range(4)] for j in range(4)]
    moments = [[abscissae[i] ** (k + 1) / (k + 1) for k in range(4)] for i in range(4)]
    tableau = table_product(moments, invert_table(vander))
    inverse = invert_table(tableau)
    running = [list(row_values) for row_values in inverse]
    coeffs = []
    for k in range(1, 5):
        trace_value = sum((running[i][i] for i in range(4)))
        coeffs.append(-trace_value / k)
        shifted_table = [
            [running[i][j] + (coeffs[-1] if i == j else 0.0) for j in range(4)] for i in range(4)
        ]
        running = table_product(inverse, shifted_table)
    start_point = (0.4, 0.9)
    estimates = [(1.0, 0.0)]
    for k in range(3):
        estimates.append(pair_mul(estimates[-1], start_point))
    for count in range(500):
        for i in range(4):
            value = (1.0, 0.0)
            for coef_value in coeffs:
                value = pair_add(pair_mul(value, estimates[i]), (coef_value, 0.0))
            denom = (1.0, 0.0)
            for j in range(4):
                if j != i:
                    denom = pair_mul(denom, pair_sub(estimates[i], estimates[j]))
            estimates[i] = pair_sub(estimates[i], pair_div(value, denom))
    chosen = [m for m in range(4) if estimates[m][1] > 0.0]
    ranking = sorted(chosen, key=lambda m: -estimates[m][1])
    columns = []
    pairs = []
    for m in ranking:
        eigen_pair = estimates[m]
        system = [
            [
                (
                    inverse[i][j] - (eigen_pair[0] if i == j else 0.0),
                    -(eigen_pair[1] if i == j else 0.0),
                )
                for j in range(4)
            ]
            for i in range(3)
        ]
        rows_left = [
            [system[i][j] for j in range(3)] + [(-system[i][3][0], -system[i][3][1])]
            for i in range(3)
        ]
        for col in range(3):
            pivot_row = max(
                range(col, 3), key=lambda r: rows_left[r][col][0] ** 2 + rows_left[r][col][1] ** 2
            )
            rows_left[col], rows_left[pivot_row] = (rows_left[pivot_row], rows_left[col])
            leading = rows_left[col][col]
            rows_left[col] = [pair_div(v, leading) for v in rows_left[col]]
            for r in range(3):
                if r != col:
                    factor = rows_left[r][col]
                    rows_left[r] = [
                        pair_sub(a, pair_mul(factor, b))
                        for a, b in zip(rows_left[r], rows_left[col])
                    ]
        vector = [rows_left[i][3] for i in range(3)] + [(1.0, 0.0)]
        columns.append([v[0] for v in vector])
        columns.append([v[1] for v in vector])
        pairs.append((eigen_pair[0], eigen_pair[1]))
    eigen_basis = [[columns[j][i] for j in range(4)] for i in range(4)]
    basis_inverse = invert_table(eigen_basis)
    return (tableau, inverse, eigen_basis, basis_inverse, pairs)


def center(padded):
    return padded[..., 1:-1, 1:-1, 1:-1]


def shifted(padded, member):
    if member == 0:
        return padded[..., 2:, 1:-1, 1:-1]
    if member == 1:
        return padded[..., :-2, 1:-1, 1:-1]
    if member == 2:
        return padded[..., 1:-1, 2:, 1:-1]
    if member == 3:
        return padded[..., 1:-1, :-2, 1:-1]
    if member == 4:
        return padded[..., 1:-1, 1:-1, 2:]
    return padded[..., 1:-1, 1:-1, :-2]


def face_terms(padded):
    middle = center(padded)
    return [0.5 * (middle + shifted(padded, m)) for m in range(6)]


def face_total(faces):
    total = faces[0]
    for m in range(1, 6):
        total = total + faces[m]
    return total


def neighbour_sum(faces, padded):
    total = faces[0] * shifted(padded, 0)
    for m in range(1, 6):
        total = total + faces[m] * shifted(padded, m)
    return total


def pad_depth(field, width):
    return jnp.pad(field, [(0, 0)] * (field.ndim - 3) + [(width, width), (0, 0), (0, 0)])


def trim_cells(field, width):
    if width == 0:
        return field
    return field[..., width:-width, width:-width, width:-width]


def apply_inverse(diag_real, coupling, determinant, vector):
    first = (diag_real * vector[0] - coupling * vector[1]) / determinant
    second = (coupling * vector[0] + diag_real * vector[1]) / determinant
    return jnp.stack([first, second])


def apply_block(diag_real, coupling, vector):
    return jnp.stack(
        [diag_real * vector[0] + coupling * vector[1], diag_real * vector[1] - coupling * vector[0]]
    )


def combine(coef, fields):
    total = coef[:, 0][:, None, None, None] * fields[0][None]
    for column in range(1, fields.shape[0]):
        total = total + coef[:, column][:, None, None, None] * fields[column][None]
    return total


def body(previous, sections, diffusivity, reaction):
    tableau, inverse, eigen_basis, basis_inverse, pairs = radau_tables()
    flux_rows = jnp.asarray(basis_inverse, jnp.float32)
    shift_table = table_product(basis_inverse, inverse)
    shift_rows = jnp.asarray(
        [[v / step_size for v in row_values] for row_values in shift_table], jnp.float32
    )
    basis_rows = jnp.asarray(eigen_basis, jnp.float32)
    pair_table = jnp.asarray([list(p) for p in pairs], jnp.float32)
    eigen_block = lax.axis_index("section")
    section_coef = diffusivity * (1.0 + 0.5 * jnp.tanh(sections))
    frozen_coef = diffusivity * (1.0 + 0.5 * jnp.tanh(previous))
    react_slope = reaction * (1.0 - 3.0 * previous * previous)
    coefs = jnp.concatenate([section_coef, frozen_coef[None], react_slope[None]], 0)
    halo_width = 1
    section_pad, coef_pad = (
        extended(sections, (("sx", 2), ("sy", 3)), halo_width),
        extended(coefs, (("sx", 2), ("sy", 3)), halo_width),
    )
    section_pad = pad_depth(section_pad, halo_width)
    coef_pad = pad_depth(coef_pad, halo_width)
    section_near = trim_cells(section_pad, halo_width - 1)
    coef_near = trim_cells(coef_pad, halo_width - 1)
    section_faces = face_terms(coef_near[:2])
    section_flux = neighbour_sum(section_faces, section_near) - face_total(section_faces) * sections
    section_flux = section_flux + reaction * sections * (1.0 - sections * sections)
    increment = sections - previous
    all_flux, all_increment = (
        lax.all_gather(section_flux, "section", axis=0, tiled=True),
        lax.all_gather(increment, "section", axis=0, tiled=True),
    )
    own_flux = lax.dynamic_slice(flux_rows, (2 * eigen_block, 0), (2, 4))
    own_shift = lax.dynamic_slice(shift_rows, (2 * eigen_block, 0), (2, 4))
    rhs = combine(own_flux, all_flux) - combine(own_shift, all_increment)
    faces_region = face_terms(coef_pad[2])
    slope_region = trim_cells(coef_pad[3], 1)
    real_part = pair_table[eigen_block, 0] / step_size
    coupling = pair_table[eigen_block, 1] / step_size
    diag_region = real_part + face_total(faces_region) - slope_region
    det_region = diag_region * diag_region + coupling * coupling
    inner_cut = halo_width - 1
    faces_inner = [trim_cells(face, inner_cut) for face in faces_region]
    diag_inner = trim_cells(diag_region, inner_cut)
    det_inner = trim_cells(det_region, inner_cut)
    residue = rhs
    correction = jnp.zeros_like(residue)
    for sweep in range(ITERS):
        scaled = apply_inverse(diag_inner, coupling, det_inner, residue)
        scaled_pad = extended(scaled, (("sx", 2), ("sy", 3)), halo_width)
        scaled_pad = pad_depth(scaled_pad, halo_width)
        search = scaled + apply_inverse(
            diag_inner, coupling, det_inner, neighbour_sum(faces_inner, scaled_pad)
        )
        search_pad = extended(search, (("sx", 2), ("sy", 3)), 1)
        search_pad = pad_depth(search_pad, 1)
        image = apply_block(diag_inner, coupling, search) - neighbour_sum(faces_inner, search_pad)
        numerator, denominator = lax.psum(
            (jnp.sum(image * residue), jnp.sum(image * image)), ("sx", "sy")
        )
        step_length = numerator / (denominator + tiny_value)
        correction = correction + step_length * search
        residue = residue - step_length * image
    gathered = lax.all_gather(correction, "section", axis=0, tiled=True)
    own_basis = lax.dynamic_slice(basis_rows, (2 * eigen_block, 0), (2, 4))
    return sections + combine(own_basis, gathered)


def solution(mesh):
    in_specs = (
        P(None, "sx", "sy"),
        P("section", None, "sx", "sy"),
        P(None, "sx", "sy"),
        P(None, "sx", "sy"),
    )
    out_specs = P("section", None, "sx", "sy")
    return jax.shard_map(body, mesh=mesh, in_specs=in_specs, out_specs=out_specs, check_vma=False)
```

profile of v0, /device:TPU:0, one launch (start us, length us, event | category | flops | bytes accessed | tf_op | source)
XLA Modules:
  0.0 365.3 jit_solution(10210758278300465663)
XLA Ops:
  7.3 8.3 %all_gather.10 = f32[4,16,16,128]{3,2,1,0:T(8,128)S(1)} all-gather(f32[2,16,16,128]{3,2,1,0:T(8,128)S(1)} %broadcast_subtract_fusion), channel_id=1, replica_groups=mesh['section'=2,'sx'=8,'sy'=2] {'section'}, dimensions={0}, use_global_device_ids=true | all-gather | bytes 786432 | tf_op jit(solution)/shard_map/all_gather | solution.py:265
  20.7 3.8 %collective-permute-start = (f32[4,16,1,128]{3,1,2,0:T(8,128)S(1)}, f32[4,16,1,128]{3,1,2,0:T(8,128)S(1)}, u32[]{:S(2)}, u32[]{:S(2)}) collective-permute-start(f32[4,16,1,128]{3,1,2,0:T(8,128)S(1)} %get-tuple-element.44), channel_id=1, source_target_pairs={{0,2},{2,4},{4,6},{6,8},{8,10},{10,12},{12,14},{1,3},{3,5},{5,7},{... | collective-permute-start | bytes 98312 | tf_op jit(solution)/shard_map/ppermute | solution.py:21
  25.9 4.6 %collective-permute-start.6 = (f32[2,16,18,1]{3,1,2,0:T(8,128)S(1)}, f32[2,16,18,1]{3,1,2,0:T(8,128)}, u32[]{:S(2)}, u32[]{:S(2)}) collective-permute-start(f32[2,16,18,1]{3,1,2,0:T(8,128)S(1)} %get-tuple-element.89), channel_id=1, source_target_pairs={{0,1},{2,3},{4,5},{6,7},{8,9},{10,11},{12,13},{14,15},{16,17},{18,... | collective-permute-start | bytes 6920 | tf_op jit(solution)/shard_map/ppermute | solution.py:21
  32.6 5.2 %collective-permute-start.2 = (f32[4,16,18,1]{2,1,3,0:T(8,128)S(1)}, f32[4,16,18,1]{2,1,3,0:T(8,128)S(1)}, u32[]{:S(2)}, u32[]{:S(2)}) collective-permute-start(f32[4,16,18,1]{2,1,3,0:T(8,128)S(1)} %copy.321), channel_id=1, source_target_pairs={{0,1},{2,3},{4,5},{6,7},{8,9},{10,11},{12,13},{14,15},{16,17},{18,... | collective-permute-start | bytes 13832 | tf_op jit(solution)/shard_map/ppermute | solution.py:21
  49.4 8.8 %all_gather.9 = f32[4,16,16,128]{3,2,1,0:T(8,128)S(1)} all-gather(f32[2,16,16,128]{3,2,1,0:T(8,128)S(1)} %copy.337), channel_id=1, replica_groups=mesh['section'=2,'sx'=8,'sy'=2] {'section'}, dimensions={0}, use_global_device_ids=true | all-gather | bytes 786432 | tf_op jit(solution)/shard_map/all_gather | solution.py:264
  65.2 4.4 %collective-permute-done.9 = f32[2,16,1,128]{3,1,2,0:T(8,128)S(1)} collective-permute-done((f32[2,16,1,128]{3,1,2,0:T(8,128)S(1)}, f32[2,16,1,128]{3,1,2,0:T(8,128)S(1)}, u32[]{:S(2)}, u32[]{:S(2)}) %collective-permute-start.9) | collective-permute-done | bytes 16416 | tf_op jit(solution)/shard_map/ppermute | solution.py:23
  69.8 3.2 collective-permute-start.10
  74.3 4.5 %collective-permute-done.10 = f32[2,16,18,1]{3,1,2,0:T(8,128)S(1)} collective-permute-done((f32[2,16,18,1]{3,1,2,0:T(8,128)S(1)}, f32[2,16,18,1]{3,1,2,0:T(8,128)S(1)}, u32[]{:S(2)}, u32[]{:S(2)}) %collective-permute-start.10) | collective-permute-done | bytes 2336 | tf_op jit(solution)/shard_map/ppermute | solution.py:21
  78.8 4.7 %collective-permute-done.11 = f32[2,16,18,1]{3,1,2,0:T(8,128)S(1)} collective-permute-done((f32[2,16,18,1]{3,1,2,0:T(8,128)S(1)}, f32[2,16,18,1]{3,1,2,0:T(8,128)S(1)}, u32[]{:S(2)}, u32[]{:S(2)}) %collective-permute-start.11) | collective-permute-done | bytes 2336 | tf_op jit(solution)/shard_map/ppermute | solution.py:23
  89.5 3.7 %collective-permute-done.13 = f32[2,16,1,128]{3,1,2,0:T(8,128)S(1)} collective-permute-done((f32[2,16,1,128]{3,1,2,0:T(8,128)S(1)}, f32[2,16,1,128]{3,1,2,0:T(8,128)S(1)}, u32[]{:S(2)}, u32[]{:S(2)}) %collective-permute-start.13) | collective-permute-done | bytes 16416 | tf_op jit(solution)/shard_map/ppermute | solution.py:23
  96.9 3.6 collective-permute-done.14
  100.5 4.7 %collective-permute-done.15 = f32[2,16,18,1]{3,1,2,0:T(8,128)S(1)} collective-permute-done((f32[2,16,18,1]{3,1,2,0:T(8,128)S(1)}, f32[2,16,18,1]{3,1,2,0:T(8,128)S(1)}, u32[]{:S(2)}, u32[]{:S(2)}) %collective-permute-start.15) | collective-permute-done | bytes 2336 | tf_op jit(solution)/shard_map/ppermute | solution.py:23
  107.6 30.2 %all-reduce.13 = (f32[]{:T(128)}, f32[]{:T(128)}) all-reduce(f32[]{:T(128)} %get-tuple-element.12, f32[]{:T(128)} %get-tuple-element.11), channel_id=1, replica_groups=mesh['section'=2,'sx'=8,'sy'=2] {'sx','sy'}, use_global_device_ids=true, to_apply=%region_1.2 | all-reduce | flops 2 | bytes 16 | tf_op jit(solution)/shard_map/psum | solution.py:292
  145.5 4.2 %collective-permute-start.18 = (f32[2,16,18,1]{3,1,2,0:T(8,128)S(1)}, f32[2,16,18,1]{3,1,2,0:T(8,128)S(1)}, u32[]{:S(2)}, u32[]{:S(2)}) collective-permute-start(f32[2,16,18,1]{3,1,2,0:T(8,128)S(1)} %get-tuple-element.83), channel_id=1, source_target_pairs={{0,1},{2,3},{4,5},{6,7},{8,9},{10,11},{12,13},{14,15},{16,17},{18,... | collective-permute-start | bytes 6920 | tf_op jit(solution)/shard_map/ppermute | solution.py:21
  151.0 5.3 %collective-permute-done.18 = f32[2,16,18,1]{3,1,2,0:T(8,128)S(1)} collective-permute-done((f32[2,16,18,1]{3,1,2,0:T(8,128)S(1)}, f32[2,16,18,1]{3,1,2,0:T(8,128)S(1)}, u32[]{:S(2)}, u32[]{:S(2)}) %collective-permute-start.18) | collective-permute-done | bytes 2336 | tf_op jit(solution)/shard_map/ppermute | solution.py:21
  156.2 4.1 %collective-permute-done.19 = f32[2,16,18,1]{3,1,2,0:T(8,128)S(1)} collective-permute-done((f32[2,16,18,1]{3,1,2,0:T(8,128)S(1)}, f32[2,16,18,1]{3,1,2,0:T(8,128)S(1)}, u32[]{:S(2)}, u32[]{:S(2)}) %collective-permute-start.19) | collective-permute-done | bytes 2336 | tf_op jit(solution)/shard_map/ppermute | solution.py:23
  170.2 4.4 %collective-permute-done.22 = f32[2,16,18,1]{3,1,2,0:T(8,128)S(1)} collective-permute-done((f32[2,16,18,1]{3,1,2,0:T(8,128)S(1)}, f32[2,16,18,1]{3,1,2,0:T(8,128)S(1)}, u32[]{:S(2)}, u32[]{:S(2)}) %collective-permute-start.22) | collective-permute-done | bytes 2336 | tf_op jit(solution)/shard_map/ppermute | solution.py:21
  174.7 4.7 %collective-permute-done.23 = f32[2,16,18,1]{3,1,2,0:T(8,128)S(1)} collective-permute-done((f32[2,16,18,1]{3,1,2,0:T(8,128)S(1)}, f32[2,16,18,1]{3,1,2,0:T(8,128)S(1)}, u32[]{:S(2)}, u32[]{:S(2)}) %collective-permute-start.23) | collective-permute-done | bytes 2336 | tf_op jit(solution)/shard_map/ppermute | solution.py:23
  180.9 30.2 %all-reduce.12 = (f32[]{:T(128)}, f32[]{:T(128)}) all-reduce(f32[]{:T(128)} %get-tuple-element.10, f32[]{:T(128)} %get-tuple-element.9), channel_id=1, replica_groups=mesh['section'=2,'sx'=8,'sy'=2] {'sx','sy'}, use_global_device_ids=true, to_apply=%region_5.6 | all-reduce | flops 2 | bytes 16 | tf_op jit(solution)/shard_map/psum | solution.py:292
  217.8 4.2 %collective-permute-start.26 = (f32[2,16,18,1]{3,1,2,0:T(8,128)S(1)}, f32[2,16,18,1]{3,1,2,0:T(8,128)S(1)}, u32[]{:S(2)}, u32[]{:S(2)}) collective-permute-start(f32[2,16,18,1]{3,1,2,0:T(8,128)S(1)} %get-tuple-element.79), channel_id=1, source_target_pairs={{0,1},{2,3},{4,5},{6,7},{8,9},{10,11},{12,13},{14,15},{16,17},{18,... | collective-permute-start | bytes 6920 | tf_op jit(solution)/shard_map/ppermute | solution.py:21
  223.3 5.3 %collective-permute-done.26 = f32[2,16,18,1]{3,1,2,0:T(8,128)S(1)} collective-permute-done((f32[2,16,18,1]{3,1,2,0:T(8,128)S(1)}, f32[2,16,18,1]{3,1,2,0:T(8,128)S(1)}, u32[]{:S(2)}, u32[]{:S(2)}) %collective-permute-start.26) | collective-permute-done | bytes 2336 | tf_op jit(solution)/shard_map/ppermute | solution.py:21
  228.5 4.1 %collective-permute-done.27 = f32[2,16,18,1]{3,1,2,0:T(8,128)S(1)} collective-permute-done((f32[2,16,18,1]{3,1,2,0:T(8,128)S(1)}, f32[2,16,18,1]{3,1,2,0:T(8,128)S(1)}, u32[]{:S(2)}, u32[]{:S(2)}) %collective-permute-start.27) | collective-permute-done | bytes 2336 | tf_op jit(solution)/shard_map/ppermute | solution.py:23
  242.4 4.6 %collective-permute-done.30 = f32[2,16,18,1]{3,1,2,0:T(8,128)S(1)} collective-permute-done((f32[2,16,18,1]{3,1,2,0:T(8,128)S(1)}, f32[2,16,18,1]{3,1,2,0:T(8,128)S(1)}, u32[]{:S(2)}, u32[]{:S(2)}) %collective-permute-start.30) | collective-permute-done | bytes 2336 | tf_op jit(solution)/shard_map/ppermute | solution.py:21
  247.0 4.7 %collective-permute-done.31 = f32[2,16,18,1]{3,1,2,0:T(8,128)S(1)} collective-permute-done((f32[2,16,18,1]{3,1,2,0:T(8,128)S(1)}, f32[2,16,18,1]{3,1,2,0:T(8,128)S(1)}, u32[]{:S(2)}, u32[]{:S(2)}) %collective-permute-start.31) | collective-permute-done | bytes 2336 | tf_op jit(solution)/shard_map/ppermute | solution.py:23
  253.2 30.2 %all-reduce.11 = (f32[]{:T(128)}, f32[]{:T(128)}) all-reduce(f32[]{:T(128)} %get-tuple-element.8, f32[]{:T(128)} %get-tuple-element.7), channel_id=1, replica_groups=mesh['section'=2,'sx'=8,'sy'=2] {'sx','sy'}, use_global_device_ids=true, to_apply=%region_9.10 | all-reduce | flops 2 | bytes 16 | tf_op jit(solution)/shard_map/psum | solution.py:292
  290.1 4.2 %collective-permute-start.34 = (f32[2,16,18,1]{3,1,2,0:T(8,128)S(1)}, f32[2,16,18,1]{3,1,2,0:T(8,128)S(1)}, u32[]{:S(2)}, u32[]{:S(2)}) collective-permute-start(f32[2,16,18,1]{3,1,2,0:T(8,128)S(1)} %get-tuple-element.75), channel_id=1, source_target_pairs={{0,1},{2,3},{4,5},{6,7},{8,9},{10,11},{12,13},{14,15},{16,17},{18,... | collective-permute-start | bytes 6920 | tf_op jit(solution)/shard_map/ppermute | solution.py:21
  295.7 5.2 %collective-permute-done.34 = f32[2,16,18,1]{3,1,2,0:T(8,128)S(1)} collective-permute-done((f32[2,16,18,1]{3,1,2,0:T(8,128)S(1)}, f32[2,16,18,1]{3,1,2,0:T(8,128)S(1)}, u32[]{:S(2)}, u32[]{:S(2)}) %collective-permute-start.34) | collective-permute-done | bytes 2336 | tf_op jit(solution)/shard_map/ppermute | solution.py:21
  300.9 4.1 %collective-permute-done.35 = f32[2,16,18,1]{3,1,2,0:T(8,128)S(1)} collective-permute-done((f32[2,16,18,1]{3,1,2,0:T(8,128)S(1)}, f32[2,16,18,1]{3,1,2,0:T(8,128)S(1)}, u32[]{:S(2)}, u32[]{:S(2)}) %collective-permute-start.35) | collective-permute-done | bytes 2336 | tf_op jit(solution)/shard_map/ppermute | solution.py:23
  314.7 4.6 %collective-permute-done.38 = f32[2,16,18,1]{3,1,2,0:T(8,128)S(1)} collective-permute-done((f32[2,16,18,1]{3,1,2,0:T(8,128)S(1)}, f32[2,16,18,1]{3,1,2,0:T(8,128)S(1)}, u32[]{:S(2)}, u32[]{:S(2)}) %collective-permute-start.38) | collective-permute-done | bytes 2336 | tf_op jit(solution)/shard_map/ppermute | solution.py:21
  319.3 4.7 %collective-permute-done.39 = f32[2,16,18,1]{3,1,2,0:T(8,128)S(1)} collective-permute-done((f32[2,16,18,1]{3,1,2,0:T(8,128)S(1)}, f32[2,16,18,1]{3,1,2,0:T(8,128)S(1)}, u32[]{:S(2)}, u32[]{:S(2)}) %collective-permute-start.39) | collective-permute-done | bytes 2336 | tf_op jit(solution)/shard_map/ppermute | solution.py:23
  325.5 30.2 %all-reduce.10 = (f32[]{:T(128)}, f32[]{:T(128)}) all-reduce(f32[]{:T(128)} %get-tuple-element.6, f32[]{:T(128)} %get-tuple-element.5), channel_id=1, replica_groups=mesh['section'=2,'sx'=8,'sy'=2] {'sx','sy'}, use_global_device_ids=true, to_apply=%region_13.14 | all-reduce | flops 2 | bytes 16 | tf_op jit(solution)/shard_map/psum | solution.py:292
  357.3 7.1 %all_gather.11 = f32[4,16,16,128]{3,2,1,0:T(8,128)S(1)} all-gather(f32[2,16,16,128]{3,2,1,0:T(8,128)S(1)} %copy.346), channel_id=1, replica_groups=mesh['section'=2,'sx'=8,'sy'=2] {'section'}, dimensions={0}, use_global_device_ids=true | all-gather | bytes 786432 | tf_op jit(solution)/shard_map/all_gather | solution.py:298
  (190 shorter events, 101.7 us)
Async XLA Ops:
  1.8 18.7 %collective-permute-start.4 = (f32[2,16,1,128]{3,1,2,0:T(8,128)S(1)}, f32[2,16,1,128]{3,1,2,0:T(8,128)S(1)}, u32[]{:S(2)}, u32[]{:S(2)}) collective-permute-start(f32[2,16,1,128]{3,1,2,0:T(8,128)S(1)} %get-tuple-element.109), channel_id=1, source_target_pairs={{0,2},{2,4},{4,6},{6,8},{8,10},{10,12},{12,14},{1,3},{3,5},{5,7},{... | collective-permute-start | bytes 49160 | tf_op jit(solution)/shard_map/ppermute | solution.py:21
  4.2 21.6 %collective-permute-start.5 = (f32[2,16,1,128]{3,1,2,0:T(8,128)S(1)}, f32[2,16,1,128]{3,1,2,0:T(8,128)S(1)}, u32[]{:S(2)}, u32[]{:S(2)}) collective-permute-start(f32[2,16,1,128]{3,1,2,0:T(8,128)S(1)} %get-tuple-element.108), channel_id=1, source_target_pairs={{2,0},{4,2},{6,4},{8,6},{10,8},{12,10},{14,12},{3,1},{5,3},{7,5},{... | collective-permute-start | bytes 49160 | tf_op jit(solution)/shard_map/ppermute | solution.py:23
  20.7 11.2 %collective-permute-start = (f32[4,16,1,128]{3,1,2,0:T(8,128)S(1)}, f32[4,16,1,128]{3,1,2,0:T(8,128)S(1)}, u32[]{:S(2)}, u32[]{:S(2)}) collective-permute-start(f32[4,16,1,128]{3,1,2,0:T(8,128)S(1)} %get-tuple-element.44), channel_id=1, source_target_pairs={{0,2},{2,4},{4,6},{6,8},{8,10},{10,12},{12,14},{1,3},{3,5},{5,7},{... | collective-permute-start | bytes 98312 | tf_op jit(solution)/shard_map/ppermute | solution.py:21
  24.5 7.4 %collective-permute-start.1 = (f32[4,16,1,128]{3,1,2,0:T(8,128)S(1)}, f32[4,16,1,128]{3,1,2,0:T(8,128)S(1)}, u32[]{:S(2)}, u32[]{:S(2)}) collective-permute-start(f32[4,16,1,128]{3,1,2,0:T(8,128)S(1)} %get-tuple-element.45), channel_id=1, source_target_pairs={{2,0},{4,2},{6,4},{8,6},{10,8},{12,10},{14,12},{3,1},{5,3},{7,5},{... | collective-permute-start | bytes 98312 | tf_op jit(solution)/shard_map/ppermute | solution.py:23
  25.9 13.7 %collective-permute-start.6 = (f32[2,16,18,1]{3,1,2,0:T(8,128)S(1)}, f32[2,16,18,1]{3,1,2,0:T(8,128)}, u32[]{:S(2)}, u32[]{:S(2)}) collective-permute-start(f32[2,16,18,1]{3,1,2,0:T(8,128)S(1)} %get-tuple-element.89), channel_id=1, source_target_pairs={{0,1},{2,3},{4,5},{6,7},{8,9},{10,11},{12,13},{14,15},{16,17},{18,... | collective-permute-start | bytes 6920 | tf_op jit(solution)/shard_map/ppermute | solution.py:21
  30.6 9.1 %collective-permute-start.7 = (f32[2,16,18,1]{3,1,2,0:T(8,128)S(1)}, f32[2,16,18,1]{3,1,2,0:T(8,128)}, u32[]{:S(2)}, u32[]{:S(2)}) collective-permute-start(f32[2,16,18,1]{3,1,2,0:T(8,128)S(1)} %get-tuple-element.88), channel_id=1, source_target_pairs={{1,0},{3,2},{5,4},{7,6},{9,8},{11,10},{13,12},{15,14},{17,16},{19,... | collective-permute-start | bytes 6920 | tf_op jit(solution)/shard_map/ppermute | solution.py:23
  32.6 8.5 %collective-permute-start.2 = (f32[4,16,18,1]{2,1,3,0:T(8,128)S(1)}, f32[4,16,18,1]{2,1,3,0:T(8,128)S(1)}, u32[]{:S(2)}, u32[]{:S(2)}) collective-permute-start(f32[4,16,18,1]{2,1,3,0:T(8,128)S(1)} %copy.321), channel_id=1, source_target_pairs={{0,1},{2,3},{4,5},{6,7},{8,9},{10,11},{12,13},{14,15},{16,17},{18,... | collective-permute-start | bytes 13832 | tf_op jit(solution)/shard_map/ppermute | solution.py:21
  38.4 5.9 %collective-permute-start.3 = (f32[4,16,18,1]{2,1,3,0:T(8,128)S(1)}, f32[4,16,18,1]{2,1,3,0:T(8,128)}, u32[]{:S(2)}, u32[]{:S(2)}) collective-permute-start(f32[4,16,18,1]{2,1,3,0:T(8,128)S(1)} %copy.322), channel_id=1, source_target_pairs={{1,0},{3,2},{5,4},{7,6},{9,8},{11,10},{13,12},{15,14},{17,16},{19,... | collective-permute-start | bytes 13832 | tf_op jit(solution)/shard_map/ppermute | solution.py:23
  61.1 4.1 %collective-permute-start.8 = (f32[2,16,1,128]{3,1,2,0:T(8,128)S(1)}, f32[2,16,1,128]{3,1,2,0:T(8,128)S(1)}, u32[]{:S(2)}, u32[]{:S(2)}) collective-permute-start(f32[2,16,1,128]{3,1,2,0:T(8,128)S(1)} %get-tuple-element.104), channel_id=1, source_target_pairs={{0,2},{2,4},{4,6},{6,8},{8,10},{10,12},{12,14},{1,3},{3,5},{5,7},{... | collective-permute-start | bytes 49160 | tf_op jit(solution)/shard_map/ppermute | solution.py:21
  63.9 5.7 %collective-permute-start.9 = (f32[2,16,1,128]{3,1,2,0:T(8,128)S(1)}, f32[2,16,1,128]{3,1,2,0:T(8,128)S(1)}, u32[]{:S(2)}, u32[]{:S(2)}) collective-permute-start(f32[2,16,1,128]{3,1,2,0:T(8,128)S(1)} %get-tuple-element.105), channel_id=1, source_target_pairs={{2,0},{4,2},{6,4},{8,6},{10,8},{12,10},{14,12},{3,1},{5,3},{7,5},{... | collective-permute-start | bytes 49160 | tf_op jit(solution)/shard_map/ppermute | solution.py:23
  69.8 9.0 %collective-permute-start.10 = (f32[2,16,18,1]{3,1,2,0:T(8,128)S(1)}, f32[2,16,18,1]{3,1,2,0:T(8,128)S(1)}, u32[]{:S(2)}, u32[]{:S(2)}) collective-permute-start(f32[2,16,18,1]{3,1,2,0:T(8,128)S(1)} %get-tuple-element.87), channel_id=1, source_target_pairs={{0,1},{2,3},{4,5},{6,7},{8,9},{10,11},{12,13},{14,15},{16,17},{18,... | collective-permute-start | bytes 6920 | tf_op jit(solution)/shard_map/ppermute | solution.py:21
  73.0 10.5 %collective-permute-start.11 = (f32[2,16,18,1]{3,1,2,0:T(8,128)S(1)}, f32[2,16,18,1]{3,1,2,0:T(8,128)S(1)}, u32[]{:S(2)}, u32[]{:S(2)}) collective-permute-start(f32[2,16,18,1]{3,1,2,0:T(8,128)S(1)} %get-tuple-element.86), channel_id=1, source_target_pairs={{1,0},{3,2},{5,4},{7,6},{9,8},{11,10},{13,12},{15,14},{17,16},{19,... | collective-permute-start | bytes 6920 | tf_op jit(solution)/shard_map/ppermute | solution.py:23
  85.2 4.3 %collective-permute-start.12 = (f32[2,16,1,128]{3,1,2,0:T(8,128)S(1)}, f32[2,16,1,128]{3,1,2,0:T(8,128)S(1)}, u32[]{:S(2)}, u32[]{:S(2)}) collective-permute-start(f32[2,16,1,128]{3,1,2,0:T(8,128)S(1)} %get-tuple-element.102), channel_id=1, source_target_pairs={{0,2},{2,4},{4,6},{6,8},{8,10},{10,12},{12,14},{1,3},{3,5},{5,7},{... | collective-permute-start | bytes 49160 | tf_op jit(solution)/shard_map/ppermute | solution.py:21
  88.2 5.0 %collective-permute-start.13 = (f32[2,16,1,128]{3,1,2,0:T(8,128)S(1)}, f32[2,16,1,128]{3,1,2,0:T(8,128)S(1)}, u32[]{:S(2)}, u32[]{:S(2)}) collective-permute-start(f32[2,16,1,128]{3,1,2,0:T(8,128)S(1)} %get-tuple-element.103), channel_id=1, source_target_pairs={{2,0},{4,2},{6,4},{8,6},{10,8},{12,10},{14,12},{3,1},{5,3},{7,5},{... | collective-permute-start | bytes 49160 | tf_op jit(solution)/shard_map/ppermute | solution.py:23
  93.4 7.1 %collective-permute-start.14 = (f32[2,16,18,1]{3,1,2,0:T(8,128)S(1)}, f32[2,16,18,1]{3,1,2,0:T(8,128)S(1)}, u32[]{:S(2)}, u32[]{:S(2)}) collective-permute-start(f32[2,16,18,1]{3,1,2,0:T(8,128)S(1)} %get-tuple-element.85), channel_id=1, source_target_pairs={{0,1},{2,3},{4,5},{6,7},{8,9},{10,11},{12,13},{14,15},{16,17},{18,... | collective-permute-start | bytes 6920 | tf_op jit(solution)/shard_map/ppermute | solution.py:21
  94.8 10.4 %collective-permute-start.15 = (f32[2,16,18,1]{3,1,2,0:T(8,128)S(1)}, f32[2,16,18,1]{3,1,2,0:T(8,128)S(1)}, u32[]{:S(2)}, u32[]{:S(2)}) collective-permute-start(f32[2,16,18,1]{3,1,2,0:T(8,128)S(1)} %get-tuple-element.84), channel_id=1, source_target_pairs={{1,0},{3,2},{5,4},{7,6},{9,8},{11,10},{13,12},{15,14},{17,16},{19,... | collective-permute-start | bytes 6920 | tf_op jit(solution)/shard_map/ppermute | solution.py:23
  142.2 3.1 collective-permute-start.17
  145.5 10.8 %collective-permute-start.18 = (f32[2,16,18,1]{3,1,2,0:T(8,128)S(1)}, f32[2,16,18,1]{3,1,2,0:T(8,128)S(1)}, u32[]{:S(2)}, u32[]{:S(2)}) collective-permute-start(f32[2,16,18,1]{3,1,2,0:T(8,128)S(1)} %get-tuple-element.83), channel_id=1, source_target_pairs={{0,1},{2,3},{4,5},{6,7},{8,9},{10,11},{12,13},{14,15},{16,17},{18,... | collective-permute-start | bytes 6920 | tf_op jit(solution)/shard_map/ppermute | solution.py:21
  149.7 10.7 %collective-permute-start.19 = (f32[2,16,18,1]{3,1,2,0:T(8,128)S(1)}, f32[2,16,18,1]{3,1,2,0:T(8,128)S(1)}, u32[]{:S(2)}, u32[]{:S(2)}) collective-permute-start(f32[2,16,18,1]{3,1,2,0:T(8,128)S(1)} %get-tuple-element.82), channel_id=1, source_target_pairs={{1,0},{3,2},{5,4},{7,6},{9,8},{11,10},{13,12},{15,14},{17,16},{19,... | collective-permute-start | bytes 6920 | tf_op jit(solution)/shard_map/ppermute | solution.py:23
  163.3 3.1 collective-permute-start.21
  166.6 8.1 %collective-permute-start.22 = (f32[2,16,18,1]{3,1,2,0:T(8,128)S(1)}, f32[2,16,18,1]{3,1,2,0:T(8,128)S(1)}, u32[]{:S(2)}, u32[]{:S(2)}) collective-permute-start(f32[2,16,18,1]{3,1,2,0:T(8,128)S(1)} %get-tuple-element.81), channel_id=1, source_target_pairs={{0,1},{2,3},{4,5},{6,7},{8,9},{10,11},{12,13},{14,15},{16,17},{18,... | collective-permute-start | bytes 6920 | tf_op jit(solution)/shard_map/ppermute | solution.py:21
  168.0 11.3 %collective-permute-start.23 = (f32[2,16,18,1]{3,1,2,0:T(8,128)S(1)}, f32[2,16,18,1]{3,1,2,0:T(8,128)S(1)}, u32[]{:S(2)}, u32[]{:S(2)}) collective-permute-start(f32[2,16,18,1]{3,1,2,0:T(8,128)S(1)} %get-tuple-element.80), channel_id=1, source_target_pairs={{1,0},{3,2},{5,4},{7,6},{9,8},{11,10},{13,12},{15,14},{17,16},{19,... | collective-permute-start | bytes 6920 | tf_op jit(solution)/shard_map/ppermute | solution.py:23
  217.8 10.8 %collective-permute-start.26 = (f32[2,16,18,1]{3,1,2,0:T(8,128)S(1)}, f32[2,16,18,1]{3,1,2,0:T(8,128)S(1)}, u32[]{:S(2)}, u32[]{:S(2)}) collective-permute-start(f32[2,16,18,1]{3,1,2,0:T(8,128)S(1)} %get-tuple-element.79), channel_id=1, source_target_pairs={{0,1},{2,3},{4,5},{6,7},{8,9},{10,11},{12,13},{14,15},{16,17},{18,... | collective-permute-start | bytes 6920 | tf_op jit(solution)/shard_map/ppermute | solution.py:21
  222.0 10.7 %collective-permute-start.27 = (f32[2,16,18,1]{3,1,2,0:T(8,128)S(1)}, f32[2,16,18,1]{3,1,2,0:T(8,128)S(1)}, u32[]{:S(2)}, u32[]{:S(2)}) collective-permute-start(f32[2,16,18,1]{3,1,2,0:T(8,128)S(1)} %get-tuple-element.78), channel_id=1, source_target_pairs={{1,0},{3,2},{5,4},{7,6},{9,8},{11,10},{13,12},{15,14},{17,16},{19,... | collective-permute-start | bytes 6920 | tf_op jit(solution)/shard_map/ppermute | solution.py:23
  235.6 3.1 collective-permute-start.29
  238.9 8.1 %collective-permute-start.30 = (f32[2,16,18,1]{3,1,2,0:T(8,128)S(1)}, f32[2,16,18,1]{3,1,2,0:T(8,128)S(1)}, u32[]{:S(2)}, u32[]{:S(2)}) collective-permute-start(f32[2,16,18,1]{3,1,2,0:T(8,128)S(1)} %get-tuple-element.77), channel_id=1, source_target_pairs={{0,1},{2,3},{4,5},{6,7},{8,9},{10,11},{12,13},{14,15},{16,17},{18,... | collective-permute-start | bytes 6920 | tf_op jit(solution)/shard_map/ppermute | solution.py:21
  240.4 11.3 %collective-permute-start.31 = (f32[2,16,18,1]{3,1,2,0:T(8,128)S(1)}, f32[2,16,18,1]{3,1,2,0:T(8,128)S(1)}, u32[]{:S(2)}, u32[]{:S(2)}) collective-permute-start(f32[2,16,18,1]{3,1,2,0:T(8,128)S(1)} %get-tuple-element.76), channel_id=1, source_target_pairs={{1,0},{3,2},{5,4},{7,6},{9,8},{11,10},{13,12},{15,14},{17,16},{19,... | collective-permute-start | bytes 6920 | tf_op jit(solution)/shard_map/ppermute | solution.py:23
  286.8 3.1 collective-permute-start.33
  290.1 10.8 %collective-permute-start.34 = (f32[2,16,18,1]{3,1,2,0:T(8,128)S(1)}, f32[2,16,18,1]{3,1,2,0:T(8,128)S(1)}, u32[]{:S(2)}, u32[]{:S(2)}) collective-permute-start(f32[2,16,18,1]{3,1,2,0:T(8,128)S(1)} %get-tuple-element.75), channel_id=1, source_target_pairs={{0,1},{2,3},{4,5},{6,7},{8,9},{10,11},{12,13},{14,15},{16,17},{18,... | collective-permute-start | bytes 6920 | tf_op jit(solution)/shard_map/ppermute | solution.py:21
  294.3 10.7 %collective-permute-start.35 = (f32[2,16,18,1]{3,1,2,0:T(8,128)S(1)}, f32[2,16,18,1]{3,1,2,0:T(8,128)S(1)}, u32[]{:S(2)}, u32[]{:S(2)}) collective-permute-start(f32[2,16,18,1]{3,1,2,0:T(8,128)S(1)} %get-tuple-element.74), channel_id=1, source_target_pairs={{1,0},{3,2},{5,4},{7,6},{9,8},{11,10},{13,12},{15,14},{17,16},{19,... | collective-permute-start | bytes 6920 | tf_op jit(solution)/shard_map/ppermute | solution.py:23
  311.2 8.1 %collective-permute-start.38 = (f32[2,16,18,1]{3,1,2,0:T(8,128)S(1)}, f32[2,16,18,1]{3,1,2,0:T(8,128)S(1)}, u32[]{:S(2)}, u32[]{:S(2)}) collective-permute-start(f32[2,16,18,1]{3,1,2,0:T(8,128)S(1)} %get-tuple-element.73), channel_id=1, source_target_pairs={{0,1},{2,3},{4,5},{6,7},{8,9},{10,11},{12,13},{14,15},{16,17},{18,... | collective-permute-start | bytes 6920 | tf_op jit(solution)/shard_map/ppermute | solution.py:21
  312.7 11.3 %collective-permute-start.39 = (f32[2,16,18,1]{3,1,2,0:T(8,128)S(1)}, f32[2,16,18,1]{3,1,2,0:T(8,128)S(1)}, u32[]{:S(2)}, u32[]{:S(2)}) collective-permute-start(f32[2,16,18,1]{3,1,2,0:T(8,128)S(1)} %get-tuple-element.72), channel_id=1, source_target_pairs={{1,0},{3,2},{5,4},{7,6},{9,8},{11,10},{13,12},{15,14},{17,16},{19,... | collective-permute-start | bytes 6920 | tf_op jit(solution)/shard_map/ppermute | solution.py:23
  (25 other events, 234.1 us)
where the time goes:
time: 367 us; the launch traced here: 365 us
  blocking collectives  145 us (40%)
  waiting for transfers between devices  94.8 us (26%)
  starting transfers between devices  77.2 us (21%)
  other arithmetic  29.6 us (8%)
  local copies, waits for them, and re-layouts  11.1 us (3%)
  between operations  7.7 us (2%)
    psum x4, blocking collectives, body(): lax.psum((jnp.sum(image * residue), jnp.sum(image * image)), ('sx', 'sy'))  121 us
    ppermute x20, waiting for transfers between devices, extended(): lax.ppermute(head, axis, [((i + 1) % count, i) for i in range(ends)])  57.3 us
    ppermute x20, starting transfers between devices, extended(): lax.ppermute(tail, axis, [(i, (i + 1) % count) for i in range(ends)])  51.2 us
    ppermute x20, waiting for transfers between devices, extended(): lax.ppermute(tail, axis, [(i, (i + 1) % count) for i in range(ends)])  37.5 us
    ppermute x20, starting transfers between devices, extended(): lax.ppermute(head, axis, [((i + 1) % count, i) for i in range(ends)])  26 us
    all_gather x1, blocking collectives, body(): lax.all_gather(section_flux, 'section', axis=0, tiled=True)  8.79 us
    all_gather x1, blocking collectives, body(): lax.all_gather(increment, 'section', axis=0, tiled=True)  8.27 us
    another operation x13, other arithmetic, apply_inverse(): return jnp.stack([first, second])  7.55 us
  transfers between devices with their start and end apart: 40, of which 25 were waited for; matrix products, arithmetic and copies ran while one was open for 3% of the time, Pallas kernels for 0%

commit v1 on v0

v1 whole, which is shorter than its diff:
```python
import functools

import jax
import jax.numpy as jnp
from jax import lax
from jax.experimental import pallas as pl
from jax.experimental.pallas import tpu as pltpu
from jax.sharding import PartitionSpec as P

ITERS = 4
DEPTH = 2 * ITERS
MESH = pl.DeviceIdType.MESH

step_size = 1.0
tiny_value = 1e-06


def invert_table(matrix):
    order_n = len(matrix)
    augmented = [
        list(matrix[r]) + [1.0 if c == r else 0.0 for c in range(order_n)] for r in range(order_n)
    ]
    for col in range(order_n):
        pivot_row = max(range(col, order_n), key=lambda r: abs(augmented[r][col]))
        augmented[col], augmented[pivot_row] = (augmented[pivot_row], augmented[col])
        leading = augmented[col][col]
        augmented[col] = [v / leading for v in augmented[col]]
        for r in range(order_n):
            if r != col:
                factor = augmented[r][col]
                augmented[r] = [a - factor * b for a, b in zip(augmented[r], augmented[col])]
    return [row_values[order_n:] for row_values in augmented]


def table_product(left, right):
    return [
        [sum((left[i][k] * right[k][j] for k in range(len(right)))) for j in range(len(right[0]))]
        for i in range(len(left))
    ]


def pair_add(first, second):
    return (first[0] + second[0], first[1] + second[1])


def pair_sub(first, second):
    return (first[0] - second[0], first[1] - second[1])


def pair_mul(first, second):
    return (
        first[0] * second[0] - first[1] * second[1],
        first[0] * second[1] + first[1] * second[0],
    )


def pair_div(first, second):
    scale_sq = second[0] * second[0] + second[1] * second[1]
    return (
        (first[0] * second[0] + first[1] * second[1]) / scale_sq,
        (first[1] * second[0] - first[0] * second[1]) / scale_sq,
    )


def quartic_value(point):
    return (((210.0 * point - 480.0) * point + 360.0) * point - 96.0) * point + 6.0


def bisect_root(lower, upper):
    for count in range(200):
        middle = 0.5 * (lower + upper)
        if (quartic_value(lower) < 0.0) == (quartic_value(middle) < 0.0):
            lower = middle
        else:
            upper = middle
    return 0.5 * (lower + upper)


def radau_tables():
    abscissae = []
    grid_steps = 4000
    for m in range(grid_steps):
        lower = 0.999 * m / grid_steps
        upper = 0.999 * (m + 1) / grid_steps
        if (quartic_value(lower) < 0.0) != (quartic_value(upper) < 0.0):
            abscissae.append(bisect_root(lower, upper))
    abscissae.append(1.0)
    vander = [[abscissae[j] ** k for k in range(4)] for j in range(4)]
    moments = [[abscissae[i] ** (k + 1) / (k + 1) for k in range(4)] for i in range(4)]
    tableau = table_product(moments, invert_table(vander))
    inverse = invert_table(tableau)
    running = [list(row_values) for row_values in inverse]
    coeffs = []
    for k in range(1, 5):
        trace_value = sum((running[i][i] for i in range(4)))
        coeffs.append(-trace_value / k)
        shifted_table = [
            [running[i][j] + (coeffs[-1] if i == j else 0.0) for j in range(4)] for i in range(4)
        ]
        running = table_product(inverse, shifted_table)
    start_point = (0.4, 0.9)
    estimates = [(1.0, 0.0)]
    for k in range(3):
        estimates.append(pair_mul(estimates[-1], start_point))
    for count in range(500):
        for i in range(4):
            value = (1.0, 0.0)
            for coef_value in coeffs:
                value = pair_add(pair_mul(value, estimates[i]), (coef_value, 0.0))
            denom = (1.0, 0.0)
            for j in range(4):
                if j != i:
                    denom = pair_mul(denom, pair_sub(estimates[i], estimates[j]))
            estimates[i] = pair_sub(estimates[i], pair_div(value, denom))
    chosen = [m for m in range(4) if estimates[m][1] > 0.0]
    ranking = sorted(chosen, key=lambda m: -estimates[m][1])
    columns = []
    pairs = []
    for m in ranking:
        eigen_pair = estimates[m]
        system = [
            [
                (
                    inverse[i][j] - (eigen_pair[0] if i == j else 0.0),
                    -(eigen_pair[1] if i == j else 0.0),
                )
                for j in range(4)
            ]
            for i in range(3)
        ]
        rows_left = [
            [system[i][j] for j in range(3)] + [(-system[i][3][0], -system[i][3][1])]
            for i in range(3)
        ]
        for col in range(3):
            pivot_row = max(
                range(col, 3), key=lambda r: rows_left[r][col][0] ** 2 + rows_left[r][col][1] ** 2
            )
            rows_left[col], rows_left[pivot_row] = (rows_left[pivot_row], rows_left[col])
            leading = rows_left[col][col]
            rows_left[col] = [pair_div(v, leading) for v in rows_left[col]]
            for r in range(3):
                if r != col:
                    factor = rows_left[r][col]
                    rows_left[r] = [
                        pair_sub(a, pair_mul(factor, b))
                        for a, b in zip(rows_left[r], rows_left[col])
                    ]
        vector = [rows_left[i][3] for i in range(3)] + [(1.0, 0.0)]
        columns.append([v[0] for v in vector])
        columns.append([v[1] for v in vector])
        pairs.append((eigen_pair[0], eigen_pair[1]))
    eigen_basis = [[columns[j][i] for j in range(4)] for i in range(4)]
    basis_inverse = invert_table(eigen_basis)
    return (tableau, inverse, eigen_basis, basis_inverse, pairs)


def near(plane, member):
    if member == 0:
        return pltpu.roll(plane, plane.shape[0] - 1, 0)
    if member == 1:
        return pltpu.roll(plane, 1, 0)
    if member == 2:
        return pltpu.roll(plane, plane.shape[1] - 1, 1)
    return pltpu.roll(plane, 1, 1)


def kernel(
    sx_count, sy_count, tables,
    prev_ref, sec_ref, diff_ref, react_ref, out_ref,
    ext_a, coef_a, ext_b, faces, face_z, alpha, beta, hist, basis,
    part, part_out, part_in, corr_out, corr_in,
    pack_a, got_a, pack_b, got_b, pack_c, got_c, gram, send_sem, recv_sem, gram_send, gram_recv,
):
    depth_z, rows, lanes = prev_ref.shape
    top = DEPTH + rows
    wide = rows + 2 * DEPTH
    group = lanes // DEPTH
    sx, sy, half = lax.axis_index("sx"), lax.axis_index("sy"), lax.axis_index("section")
    q_table, c_table, p_table, pairs = tables

    def pick(first, second):
        return jnp.where(half == 0, jnp.float32(first), jnp.float32(second))

    barrier = pltpu.get_barrier_semaphore()
    members = sx_count * sy_count
    me = sx * sy_count + sy

    def member_at(offset):
        other = lax.rem(me + offset, members)
        return {"sx": other // sy_count, "sy": lax.rem(other, sy_count)}

    ext_a[...] = jnp.zeros_like(ext_a)
    ext_b[...] = jnp.zeros_like(ext_b)
    got_a[...] = jnp.zeros_like(got_a)
    got_b[...] = jnp.zeros_like(got_b)
    got_c[...] = jnp.zeros_like(got_c)
    for field in range(2):
        hist[0, field] = jnp.zeros(hist.shape[2:], jnp.float32)

    def greet(offset, carry):
        pl.semaphore_signal(barrier, inc=1, device_id=member_at(offset), device_id_type=MESH)
        return carry

    lax.fori_loop(1, members, greet, 0)
    pl.semaphore_signal(barrier, inc=1, device_id={"section": 1 - half}, device_id_type=MESH)

    lane_group = lax.broadcasted_iota(jnp.int32, (rows, lanes), 1) // DEPTH

    def pack(plane_of, low, high):
        down = jnp.zeros((rows, lanes), jnp.float32)
        up = jnp.zeros((rows, lanes), jnp.float32)
        for z in range(depth_z):
            plane = plane_of(z)
            if z > 0:
                plane = pltpu.roll(plane, DEPTH * z, 1)
            down = jnp.where(lane_group == z, plane, down)
            up = jnp.where(lane_group == (z + group - 1) % group, plane, up)
        low[...] = down
        high[...] = up

    def unpack(from_high, from_low, store):
        count = from_high.shape[0]
        groups = lax.broadcasted_iota(jnp.int32, (count, lanes), 1) // DEPTH
        zero = jnp.zeros((count, lanes), jnp.float32)
        for z in range(depth_z):
            mixed = jnp.where(
                groups == z,
                from_high,
                jnp.where(groups == (z + group - 1) % group, from_low, zero),
            )
            if z > 0:
                mixed = pltpu.roll(mixed, lanes - DEPTH * z, 1)
            store(z, mixed)

    for j in range(2):
        pack(lambda z: sec_ref[j, z], pack_a.at[0, j], pack_a.at[1, j])
        ext_a[j, 1 : depth_z + 1, DEPTH:top, 0:lanes] = sec_ref[j]
    pack(lambda z: diff_ref[z], pack_a.at[0, 2], pack_a.at[1, 2])
    ext_a[2, 1 : depth_z + 1, DEPTH:top, 0:lanes] = diff_ref[...]

    def frozen(z, carry):
        before = prev_ref[z]
        ext_b[0, z + 1, DEPTH:top, 0:lanes] = diff_ref[z] * (1.0 + 0.5 * jnp.tanh(before))
        ext_b[1, z + 1, DEPTH:top, 0:lanes] = react_ref[z] * (1.0 - 3.0 * before * before)
        return carry

    lax.fori_loop(0, depth_z, frozen, 0)
    for j in range(2):
        pack(lambda z: ext_b[j, z + 1, DEPTH:top, 0:lanes], pack_b.at[0, j], pack_b.at[1, j])

    pl.semaphore_wait(barrier, members)

    used = [0]

    def copy(source, target, device):
        at = used[0]
        used[0] += 1
        return pltpu.make_async_remote_copy(
            src_ref=source,
            dst_ref=target,
            send_sem=send_sem.at[at],
            recv_sem=recv_sem.at[at],
            device_id=device,
            device_id_type=MESH,
        )

    left, right = lax.rem(sx + sx_count - 1, sx_count), lax.rem(sx + 1, sx_count)
    below, above = lax.rem(sy + sy_count - 1, sy_count), lax.rem(sy + 1, sy_count)
    has_left, has_right = sx > 0, sx < sx_count - 1
    has_below, has_above = sy > 0, sy < sy_count - 1
    body_z = pl.ds(1, depth_z)
    own = pl.ds(0, lanes)
    low_rows, high_rows = pl.ds(0, DEPTH), pl.ds(top, DEPTH)

    def slabs(low_source, high_source, target):
        return [
            (has_left, has_right, copy(low_source, target(high_rows), {"sx": left})),
            (has_right, has_left, copy(high_source, target(low_rows), {"sx": right})),
        ]

    def strips(packed, got, corners):
        result = []
        for side, device, out_ok, in_ok in (
            (0, below, has_below, has_above),
            (1, above, has_above, has_below),
        ):
            middle = got.at[side, :, pl.ds(DEPTH, rows), :] if corners else got.at[side]
            result.append((out_ok, in_ok, copy(packed.at[side], middle, {"sy": device})))
            if corners:
                result.append((
                    out_ok & has_left,
                    in_ok & has_right,
                    copy(
                        packed.at[side, :, pl.ds(0, DEPTH), :],
                        got.at[side, :, high_rows, :],
                        {"sx": left, "sy": device},
                    ),
                ))
                result.append((
                    out_ok & has_right,
                    in_ok & has_left,
                    copy(
                        packed.at[side, :, pl.ds(rows - DEPTH, DEPTH), :],
                        got.at[side, :, low_rows, :],
                        {"sx": right, "sy": device},
                    ),
                ))
        return result

    def start(copies):
        for out_ok, in_ok, one in copies:
            pl.when(out_ok)(one.start)

    def receive(copies):
        for out_ok, in_ok, one in copies:
            pl.when(in_ok)(one.wait_recv)

    def release(copies):
        for out_ok, in_ok, one in copies:
            pl.when(out_ok)(one.wait_send)

    copies_a = strips(pack_a, got_a, False)
    copies_a += slabs(
        diff_ref.at[:, pl.ds(0, DEPTH), :],
        diff_ref.at[:, pl.ds(rows - DEPTH, DEPTH), :],
        lambda where: ext_a.at[2, body_z, where, own],
    )
    copies_a += slabs(
        sec_ref.at[:, :, pl.ds(0, DEPTH), :],
        sec_ref.at[:, :, pl.ds(rows - DEPTH, DEPTH), :],
        lambda where: ext_a.at[pl.ds(0, 2), body_z, where, own],
    )
    start(copies_a)
    copies_b = strips(pack_b, got_b, True)
    copies_b += slabs(
        ext_b.at[:, body_z, pl.ds(DEPTH, DEPTH), own],
        ext_b.at[:, body_z, pl.ds(top - DEPTH, DEPTH), own],
        lambda where: ext_b.at[:, body_z, where, own],
    )
    start(copies_b)

    receive(copies_a)

    for j in range(3):
        def put_a(z, plane):
            ext_a[j, z + 1, DEPTH:top, lanes : 2 * lanes] = plane

        unpack(got_a[0, j], got_a[1, j], put_a)

    def section_coefs(z, carry):
        for j in range(2):
            coef_a[j, z] = ext_a[2, z] * (1.0 + 0.5 * jnp.tanh(ext_a[j, z]))
        return carry

    lax.fori_loop(0, depth_z + 2, section_coefs, 0)

    q_own = [[pick(q_table[m][j], q_table[2 + m][2 + j]) for j in range(2)] for m in range(2)]
    q_far = [[pick(q_table[2 + m][j], q_table[m][2 + j]) for j in range(2)] for m in range(2)]
    c_own = [[pick(c_table[m][j], c_table[2 + m][2 + j]) for j in range(2)] for m in range(2)]
    c_far = [[pick(c_table[2 + m][j], c_table[m][2 + j]) for j in range(2)] for m in range(2)]

    def middle(plane):
        return plane[DEPTH:top, 0:lanes]

    def fluxes(z, carry):
        flux, increment = [], []
        for j in range(2):
            cells, coefs = ext_a[j, z + 1], coef_a[j, z + 1]
            here, coef_here = middle(cells), middle(coefs)
            total = jnp.zeros_like(here)
            for member in range(4):
                face = 0.5 * (coef_here + middle(near(coefs, member)))
                total = total + face * (middle(near(cells, member)) - here)
            for level in (z, z + 2):
                face = 0.5 * (coef_here + middle(coef_a[j, level]))
                total = total + face * (middle(ext_a[j, level]) - here)
            flux.append(total + react_ref[z] * here * (1.0 - here * here))
            increment.append(here - prev_ref[z])
        for m in range(2):
            part[m, z] = (
                q_own[m][0] * flux[0] + q_own[m][1] * flux[1]
                - c_own[m][0] * increment[0] - c_own[m][1] * increment[1]
            )
            part_out[m, z] = (
                q_far[m][0] * flux[0] + q_far[m][1] * flux[1]
                - c_far[m][0] * increment[0] - c_far[m][1] * increment[1]
            )
        return carry

    chunk = depth_z // 4
    swap = []
    for at in range(4):
        lax.fori_loop(at * chunk, (at + 1) * chunk, fluxes, 0)
        piece = pl.ds(at * chunk, chunk)
        one = copy(part_out.at[:, piece], part_in.at[:, piece], {"section": 1 - half})
        one.start()
        swap.append(one)

    receive(copies_b)

    for j in range(2):
        def put_b(z, plane):
            ext_b[j, z + 1, :, lanes : 2 * lanes] = plane

        unpack(got_b[0, j], got_b[1, j], put_b)

    real_part = pick(pairs[0][0] / step_size, pairs[1][0] / step_size)
    coupling = pick(pairs[0][1] / step_size, pairs[1][1] / step_size)
    row_at = lax.broadcasted_iota(jnp.int32, (wide, 2 * lanes), 0)
    lane_at = lax.broadcasted_iota(jnp.int32, (wide, 2 * lanes), 1)
    inside = ((row_at >= DEPTH) | has_left) & ((row_at < top) | has_right)
    inside = inside & (
        (lane_at < lanes)
        | ((lane_at < lanes + DEPTH) & has_above)
        | ((lane_at >= 2 * lanes - DEPTH) & has_below)
    )
    keep = inside.astype(jnp.float32)

    def depth_faces(z, carry):
        face_z[z] = 0.5 * (ext_b[0, z] + ext_b[0, z + 1])
        return carry

    lax.fori_loop(0, depth_z + 1, depth_faces, 0)

    def operator(z, carry):
        coefs = ext_b[0, z + 1]
        diag = real_part - ext_b[1, z + 1] + face_z[z] + face_z[z + 1]
        for member in range(4):
            face = 0.5 * (coefs + near(coefs, member))
            faces[member, z] = face
            diag = diag + face
        scale = keep / (diag * diag + coupling * coupling)
        alpha[z] = diag * scale
        beta[z] = coupling * scale
        return carry

    lax.fori_loop(0, depth_z, operator, 0)

    for m in range(1, DEPTH):
        for field in range(2):
            hist[m, field, 0] = jnp.zeros((wide, 2 * lanes), jnp.float32)
            hist[m, field, depth_z + 1] = jnp.zeros((wide, 2 * lanes), jnp.float32)

    for one in swap:
        one.wait_recv()

    def first_scaled(z, carry):
        rhs = [part[m, z] + part_in[m, z] for m in range(2)]
        a, b = middle(alpha[z]), middle(beta[z])
        for m in range(2):
            basis[0, m, z] = rhs[m]
        hist[0, 0, z + 1, DEPTH:top, 0:lanes] = a * rhs[0] - b * rhs[1]
        hist[0, 1, z + 1, DEPTH:top, 0:lanes] = b * rhs[0] + a * rhs[1]
        return carry

    lax.fori_loop(0, depth_z, first_scaled, 0)
    copies_c = slabs(
        hist.at[0, :, body_z, pl.ds(DEPTH, DEPTH), own],
        hist.at[0, :, body_z, pl.ds(top - DEPTH, DEPTH), own],
        lambda where: hist.at[0, :, body_z, where, own],
    )
    start(copies_c)
    for j in range(2):
        pack(lambda z: hist[0, j, z + 1, DEPTH:top, 0:lanes], pack_c.at[0, j], pack_c.at[1, j])
    more_c = strips(pack_c, got_c, True)
    start(more_c)
    copies_c = copies_c + more_c
    receive(copies_c)

    for j in range(2):
        def put_c(z, plane):
            hist[0, j, z + 1, :, lanes : 2 * lanes] = plane

        unpack(got_c[0, j], got_c[1, j], put_c)

    for m in range(DEPTH - 1):
        def apply(z, carry):
            around = []
            for field in range(2):
                cells = hist[m, field, z + 1]
                total = face_z[z] * hist[m, field, z] + face_z[z + 1] * hist[m, field, z + 2]
                for member in range(4):
                    total = total + faces[member, z] * near(cells, member)
                around.append(total)
            if m % 2 == 1:
                for field in range(2):
                    basis[(m + 1) // 2, field, z] = middle(around[field])
            a, b = alpha[z], beta[z]
            hist[m + 1, 0, z + 1] = a * around[0] - b * around[1]
            hist[m + 1, 1, z + 1] = b * around[0] + a * around[1]
            return carry

        lax.fori_loop(0, depth_z, apply, 0)

    index = [(i, j) for i in range(ITERS + 1) for j in range(i, ITERS + 1)]

    def last_apply(z, carry):
        totals = list(carry)
        for field in range(2):
            cells = hist[DEPTH - 1, field, z + 1]
            total = middle(face_z[z]) * middle(hist[DEPTH - 1, field, z])
            total = total + middle(face_z[z + 1]) * middle(hist[DEPTH - 1, field, z + 2])
            for member in range(4):
                total = total + middle(faces[member, z]) * middle(near(cells, member))
            members_of = [basis[k, field, z] for k in range(ITERS)] + [total]
            for at, (i, j) in enumerate(index):
                product = members_of[i] * members_of[j]
                for r in range(0, rows, 8):
                    totals[at] = totals[at] + product[r : r + 8]
        return tuple(totals)

    zeros = tuple(jnp.zeros((8, lanes), jnp.float32) for pair in index)
    sums = lax.fori_loop(0, depth_z, last_apply, zeros)
    gram[0, len(index) : 16] = jnp.zeros((16 - len(index), lanes), jnp.float32)
    for at, total in enumerate(sums):
        gram[0, at : at + 1] = jnp.sum(total, axis=0, keepdims=True)

    def gram_copy(offset):
        return pltpu.make_async_remote_copy(
            src_ref=gram.at[0],
            dst_ref=gram.at[offset],
            send_sem=gram_send.at[offset],
            recv_sem=gram_recv.at[offset],
            device_id=member_at(offset),
            device_id_type=MESH,
        )

    def gram_start(offset, carry):
        gram_copy(offset).start()
        return carry

    def gram_take(offset, carry):
        gram_copy(offset).wait_recv()
        return carry

    def gram_release(offset, carry):
        gram_copy(offset).wait_send()
        return carry

    lax.fori_loop(1, members, gram_start, 0)
    release(copies_a)
    release(copies_b)
    release(copies_c)
    for one in swap:
        one.wait_send()
    lax.fori_loop(1, members, gram_take, 0)
    table = gram[0]
    turn = [lax.rem(me - place + members, members) for place in range(members)]
    table = gram[turn[0]]
    for place in range(1, members):
        table = table + gram[turn[place]]
    table = jnp.sum(table, axis=1, keepdims=True)
    entry = {}
    for at, (i, j) in enumerate(index):
        entry[i, j] = entry[j, i] = table[at : at + 1, :]

    weights = {0: jnp.ones((1, 1), jnp.float32)}
    gains = {}
    for sweep in range(ITERS):
        image = {}
        for j in range(sweep + 2):
            if j in weights and j - 1 in weights:
                image[j] = weights[j] - weights[j - 1]
            elif j in weights:
                image[j] = weights[j]
            else:
                image[j] = -weights[j - 1]
        against = {
            j: functools.reduce(jnp.add, [image[i] * entry[i, j] for i in image]) for j in image
        }
        numerator = functools.reduce(jnp.add, [against[j] * weights[j] for j in weights])
        denominator = functools.reduce(jnp.add, [against[j] * image[j] for j in image])
        step = numerator / (denominator + tiny_value)
        for j in weights:
            gains[j] = gains[j] + step * weights[j] if j in gains else step * weights[j]
        weights = {
            j: (weights[j] - step * image[j]) if j in weights else -step * image[j] for j in image
        }

    p_own = [[pick(p_table[j][m], p_table[2 + j][2 + m]) for m in range(2)] for j in range(2)]
    p_far = [[pick(p_table[2 + j][m], p_table[j][2 + m]) for m in range(2)] for j in range(2)]
    gain_at = [jnp.broadcast_to(gains[k], (rows, lanes)) for k in range(ITERS)]

    def correct(z, carry):
        fix = []
        for field in range(2):
            total = None
            for k in range(ITERS):
                search = middle(hist[2 * k, field, z + 1]) + middle(hist[2 * k + 1, field, z + 1])
                total = gain_at[k] * search if total is None else total + gain_at[k] * search
            fix.append(total)
        for j in range(2):
            corr_out[j, z] = p_far[j][0] * fix[0] + p_far[j][1] * fix[1]
            part[j, z] = sec_ref[j, z] + p_own[j][0] * fix[0] + p_own[j][1] * fix[1]
        return carry

    final = []
    for at in range(4):
        lax.fori_loop(at * chunk, (at + 1) * chunk, correct, 0)
        piece = pl.ds(at * chunk, chunk)
        one = copy(corr_out.at[:, piece], corr_in.at[:, piece], {"section": 1 - half})
        one.start()
        final.append(one)
    for at in range(4):
        final[at].wait_recv()

        def finish(z, carry):
            for j in range(2):
                out_ref[j, z] = part[j, z] + corr_in[j, z]
            return carry

        lax.fori_loop(at * chunk, (at + 1) * chunk, finish, 0)
    for one in final:
        one.wait_send()
    lax.fori_loop(1, members, gram_release, 0)


def solution(mesh):
    sx_count, sy_count = mesh.shape["sx"], mesh.shape["sy"]
    tableau, inverse, eigen_basis, basis_inverse, pairs = radau_tables()
    shift_table = table_product(basis_inverse, inverse)
    shift_table = [[v / step_size for v in row_values] for row_values in shift_table]
    tables = (basis_inverse, shift_table, eigen_basis, pairs)

    def body(previous, sections, diffusivity, reaction):
        depth_z, rows, lanes = previous.shape
        wide = rows + 2 * DEPTH
        f32 = jnp.float32
        vmem = pltpu.VMEM
        ext = (depth_z + 2, wide, 2 * lanes)
        flat = (depth_z, wide, 2 * lanes)
        block = (2, depth_z, rows, lanes)
        members = sx_count * sy_count
        return pl.pallas_call(
            functools.partial(kernel, sx_count, sy_count, tables),
            out_shape=jax.ShapeDtypeStruct(sections.shape, f32),
            in_specs=[pl.BlockSpec(memory_space=pltpu.VMEM)] * 4,
            out_specs=pl.BlockSpec(memory_space=pltpu.VMEM),
            scratch_shapes=[
                vmem((3,) + ext, f32),
                vmem((2,) + ext, f32),
                vmem((2,) + ext, f32),
                vmem((4,) + flat, f32),
                vmem((depth_z + 1, wide, 2 * lanes), f32),
                vmem(flat, f32),
                vmem(flat, f32),
                vmem((DEPTH, 2) + ext, f32),
                vmem((ITERS,) + block, f32),
                vmem(block, f32),
                vmem(block, f32),
                vmem(block, f32),
                vmem(block, f32),
                vmem(block, f32),
                vmem((2, 3, rows, lanes), f32),
                vmem((2, 3, rows, lanes), f32),
                vmem((2, 2, rows, lanes), f32),
                vmem((2, 2, wide, lanes), f32),
                vmem((2, 2, rows, lanes), f32),
                vmem((2, 2, wide, lanes), f32),
                vmem((members, 16, lanes), f32),
                pltpu.SemaphoreType.DMA((32,)),
                pltpu.SemaphoreType.DMA((32,)),
                pltpu.SemaphoreType.DMA((members,)),
                pltpu.SemaphoreType.DMA((members,)),
            ],
            compiler_params=pltpu.CompilerParams(
                collective_id=0, has_side_effects=True, vmem_limit_bytes=48 * 1024 * 1024
            ),
        )(previous, sections, diffusivity, reaction)

    in_specs = (
        P(None, "sx", "sy"),
        P("section", None, "sx", "sy"),
        P(None, "sx", "sy"),
        P(None, "sx", "sy"),
    )
    out_specs = P("section", None, "sx", "sy")
    return jax.shard_map(body, mesh=mesh, in_specs=in_specs, out_specs=out_specs, check_vma=False)
```

time: 367 us -> 53.9 us (0.15)
  blocking collectives: 145 us -> 0 us
  waiting for transfers between devices: 94.8 us -> 0 us
  starting transfers between devices: 77.2 us -> 0 us
  Pallas kernels: 0 us -> 49.4 us
  other arithmetic: 29.6 us -> 0 us
  between operations: 7.7 us -> 0.01 us
  local copies, waits for them, and re-layouts: 11.1 us -> 4.37 us
    psum x4 -> x0, blocking collectives: 121 us -> none  [body(): lax.psum((jnp.sum(image * residue), jnp.sum(image * image)), ('sx', 'sy'))]
    ppermute x40 -> x0, waiting for transfers between devices: 94.8 us -> none  [the longest x20 57.3 us: extended(): lax.ppermute(head, axis, [((i + 1) % count, i) for i in range(ends)])]
    ppermute x40 -> x0, starting transfers between devices: 77.2 us -> none  [the longest x20 51.2 us: extended(): lax.ppermute(tail, axis, [(i, (i + 1) % count) for i in range(ends)])]
    pallas_call x0 -> x1, Pallas kernels: none -> 49.4 us  [body(): pl.pallas_call(functools.partial(kernel, sx_count, sy_count, tables), out...]
    all_gather x3 -> x0, blocking collectives: 24.2 us -> none  [the longest x1 8.79 us: body(): lax.all_gather(section_flux, 'section', axis=0, tiled=True)]
    another operation x17 -> x0, other arithmetic: 10.4 us -> none  [the longest x13 7.55 us: apply_inverse(): return jnp.stack([first, second])]
    concatenate x19 -> x0, other arithmetic: 5.92 us -> none  [extended(): jnp.concatenate([lax.ppermute(tail, axis, [(i, (i + 1) % count) for i in...]
    reduce_sum x4 -> x0, other arithmetic: 5.2 us -> none  [body(): jnp.sum(image * image)]
  transfers between devices with their start and end apart: 40 -> 0, of which waited for: 25 -> 0; matrix products, arithmetic and copies ran while one was open for 3% -> 0% of each run, Pallas kernels for 0% -> 0%
where the time goes in v1:
time: 53.9 us; the launch traced here: 53.7 us
  Pallas kernels  49.4 us (92%)
  local copies, waits for them, and re-layouts  4.37 us (8%)
    pallas_call x1, Pallas kernels, body(): pl.pallas_call(functools.partial(kernel, sx_count, sy_count, tables), out...  49.4 us
    unnamed x9, local copies, waits for them, and re-layouts  4.37 us

profile of v1, /device:TPU:0, one launch (start us, length us, event | category | flops | bytes accessed | tf_op | source)
XLA Modules:
  0.0 53.7 jit_solution(13053606743714942989)
XLA Ops:
  0.0 0.0 copy-start
  0.0 0.9 %copy-done = f32[2,16,16,128]{3,2,1,0:T(8,128)S(1)} copy-done((f32[2,16,16,128]{3,2,1,0:T(8,128)S(1)}, f32[2,16,16,128]{3,2,1,0:T(8,128)}, u32[]{:S(2)}) %copy-start) | copy-done | bytes 262168
  1.0 0.0 copy-start.1
  1.0 0.9 %copy-done.1 = f32[16,16,128]{2,1,0:T(8,128)S(1)} copy-done((f32[16,16,128]{2,1,0:T(8,128)S(1)}, f32[16,16,128]{2,1,0:T(8,128)}, u32[]{:S(2)}) %copy-start.1) | copy-done | bytes 131096
  1.9 0.0 copy-start.2
  1.9 0.9 %copy-done.2 = f32[16,16,128]{2,1,0:T(8,128)S(1)} copy-done((f32[16,16,128]{2,1,0:T(8,128)S(1)}, f32[16,16,128]{2,1,0:T(8,128)}, u32[]{:S(2)}) %copy-start.2) | copy-done | bytes 131096
  2.8 0.0 copy-start.3
  2.8 0.9 %copy-done.3 = f32[16,16,128]{2,1,0:T(8,128)S(1)} copy-done((f32[16,16,128]{2,1,0:T(8,128)S(1)}, f32[16,16,128]{2,1,0:T(8,128)}, u32[]{:S(2)}) %copy-start.3) | copy-done | bytes 131096
  3.7 49.4 %shard_map.46 = f32[2,16,16,128]{3,2,1,0:T(8,128)S(1)} custom-call(f32[16,16,128]{2,1,0:T(8,128)S(1)} %copy-done.1, f32[2,16,16,128]{3,2,1,0:T(8,128)S(1)} %copy-done, f32[16,16,128]{2,1,0:T(8,128)S(1)} %copy-done.2, f32[16,16,128]{2,1,0:T(8,128)S(1)} %copy-done.3), custom_call_target="tpu_custom_call" | custom-call | tf_op jit(solution)/shard_map/pallas_call | solution.py:635
  53.0 0.7 %copy.6 = f32[2,16,16,128]{3,2,1,0:T(8,128)} copy(f32[2,16,16,128]{3,2,1,0:T(8,128)S(1)} %shard_map.46) | data formatting | bytes 524288
Async XLA Ops:
  0.0 0.9 %copy-start = (f32[2,16,16,128]{3,2,1,0:T(8,128)S(1)}, f32[2,16,16,128]{3,2,1,0:T(8,128)}, u32[]{:S(2)}) copy-start(f32[2,16,16,128]{3,2,1,0:T(8,128)} %sec_ref.1) | copy-start | bytes 786436
  1.0 0.9 %copy-start.1 = (f32[16,16,128]{2,1,0:T(8,128)S(1)}, f32[16,16,128]{2,1,0:T(8,128)}, u32[]{:S(2)}) copy-start(f32[16,16,128]{2,1,0:T(8,128)} %prev_ref.1) | copy-start | bytes 393220
  1.9 0.9 %copy-start.2 = (f32[16,16,128]{2,1,0:T(8,128)S(1)}, f32[16,16,128]{2,1,0:T(8,128)}, u32[]{:S(2)}) copy-start(f32[16,16,128]{2,1,0:T(8,128)} %diff_ref.1) | copy-start | bytes 393220
  2.8 0.9 %copy-start.3 = (f32[16,16,128]{2,1,0:T(8,128)S(1)}, f32[16,16,128]{2,1,0:T(8,128)}, u32[]{:S(2)}) copy-start(f32[16,16,128]{2,1,0:T(8,128)} %react_ref.1) | copy-start | bytes 393220

commit v2 on v1

--- a/solution.py
+++ b/solution.py
@@ -167,11 +167,16 @@
 
 def kernel(
     sx_count, sy_count, tables,
-    prev_ref, sec_ref, diff_ref, react_ref, out_ref,
-    ext_a, coef_a, ext_b, faces, face_z, alpha, beta, hist, basis,
-    part, part_out, part_in, corr_out, corr_in,
-    pack_a, got_a, pack_b, got_b, pack_c, got_c, gram, send_sem, recv_sem, gram_send, gram_recv,
+    prev_any, sec_any, diff_any, react_any, out_ref,
+    prev_ref, sec_ref, diff_ref, react_ref,
+    ext_a, ext_b, faces, face_z, alpha, beta, *rest,
 ):
+    hist, rest = rest[:DEPTH], rest[DEPTH:]
+    (
+    basis, part, part_out, part_in, corr_out, corr_in,
+    pack_a, got_a, pack_b, got_b, pack_c, got_c, gram, load_sem,
+    send_sem, recv_sem, gram_send, gram_recv,
+    ) = rest
     depth_z, rows, lanes = prev_ref.shape
     top = DEPTH + rows
     wide = rows + 2 * DEPTH
@@ -190,13 +195,21 @@
         other = lax.rem(me + offset, members)
         return {"sx": other // sy_count, "sy": lax.rem(other, sy_count)}
 
+    loads = [
+        pltpu.make_async_copy(source, target, load_sem.at[at])
+        for at, (source, target) in enumerate((
+            (sec_any, sec_ref), (diff_any, diff_ref), (prev_any, prev_ref), (react_any, react_ref),
+        ))
+    ]
+    for one in loads:
+        one.start()
     ext_a[...] = jnp.zeros_like(ext_a)
     ext_b[...] = jnp.zeros_like(ext_b)
     got_a[...] = jnp.zeros_like(got_a)
     got_b[...] = jnp.zeros_like(got_b)
     got_c[...] = jnp.zeros_like(got_c)
     for field in range(2):
-        hist[0, field] = jnp.zeros(hist.shape[2:], jnp.float32)
+        hist[0][field] = jnp.zeros(hist[0].shape[1:], jnp.float32)
 
     def greet(offset, carry):
         pl.semaphore_signal(barrier, inc=1, device_id=member_at(offset), device_id_type=MESH)
@@ -233,19 +246,39 @@
                 mixed = pltpu.roll(mixed, lanes - DEPTH * z, 1)
             store(z, mixed)
 
-    for j in range(2):
-        pack(lambda z: sec_ref[j, z], pack_a.at[0, j], pack_a.at[1, j])
-        ext_a[j, 1 : depth_z + 1, DEPTH:top, 0:lanes] = sec_ref[j]
-    pack(lambda z: diff_ref[z], pack_a.at[0, 2], pack_a.at[1, 2])
-    ext_a[2, 1 : depth_z + 1, DEPTH:top, 0:lanes] = diff_ref[...]
-
-    def frozen(z, carry):
-        before = prev_ref[z]
-        ext_b[0, z + 1, DEPTH:top, 0:lanes] = diff_ref[z] * (1.0 + 0.5 * jnp.tanh(before))
-        ext_b[1, z + 1, DEPTH:top, 0:lanes] = react_ref[z] * (1.0 - 3.0 * before * before)
-        return carry
-
-    lax.fori_loop(0, depth_z, frozen, 0)
+    for one in loads:
+        one.wait()
+
+    def planes(fn, least, most, batch):
+        def several(at, carry):
+            stores = []
+            for step in range(batch):
+                stores.append(fn(least + at * batch + step))
+            for store in stores:
+                store()
+            return carry
+
+        lax.fori_loop(0, (most - least) // batch, several, 0)
+
+    def own_coefs(z):
+        before, diffusivity = prev_ref[z], diff_ref[z]
+        cells = [sec_ref[j, z] for j in range(2)]
+        coefs = [diffusivity * (1.0 + 0.5 * jnp.tanh(cells[j])) for j in range(2)]
+        coef = diffusivity * (1.0 + 0.5 * jnp.tanh(before))
+        slope = react_ref[z] * (1.0 - 3.0 * before * before)
+
+        def store():
+            for j in range(2):
+                ext_a[j, z + 1, DEPTH:top, 0:lanes] = cells[j]
+                ext_a[2 + j, z + 1, DEPTH:top, 0:lanes] = coefs[j]
+            ext_b[0, z + 1, DEPTH:top, 0:lanes] = coef
+            ext_b[1, z + 1, DEPTH:top, 0:lanes] = slope
+
+        return store
+
+    planes(own_coefs, 0, depth_z, 2)
+    for j in range(4):
+        pack(lambda z: ext_a[j, z + 1, DEPTH:top, 0:lanes], pack_a.at[0, j], pack_a.at[1, j])
     for j in range(2):
         pack(lambda z: ext_b[j, z + 1, DEPTH:top, 0:lanes], pack_b.at[0, j], pack_b.at[1, j])
 
@@ -321,16 +354,25 @@
             pl.when(out_ok)(one.wait_send)
 
     copies_a = strips(pack_a, got_a, False)
-    copies_a += slabs(
-        diff_ref.at[:, pl.ds(0, DEPTH), :],
-        diff_ref.at[:, pl.ds(rows - DEPTH, DEPTH), :],
-        lambda where: ext_a.at[2, body_z, where, own],
-    )
-    copies_a += slabs(
-        sec_ref.at[:, :, pl.ds(0, DEPTH), :],
-        sec_ref.at[:, :, pl.ds(rows - DEPTH, DEPTH), :],
-        lambda where: ext_a.at[pl.ds(0, 2), body_z, where, own],
-    )
+    edge = pl.ds(top, 1), pl.ds(DEPTH - 1, 1)
+    copies_a.append((
+        has_left,
+        has_right,
+        copy(
+            ext_a.at[:, body_z, pl.ds(DEPTH, 1), own],
+            ext_a.at[:, body_z, edge[0], own],
+            {"sx": left},
+        ),
+    ))
+    copies_a.append((
+        has_right,
+        has_left,
+        copy(
+            ext_a.at[:, body_z, pl.ds(top - 1, 1), own],
+            ext_a.at[:, body_z, edge[1], own],
+            {"sx": right},
+        ),
+    ))
     start(copies_a)
     copies_b = strips(pack_b, got_b, True)
     copies_b += slabs(
@@ -342,18 +384,11 @@
 
     receive(copies_a)
 
-    for j in range(3):
+    for j in range(4):
         def put_a(z, plane):
             ext_a[j, z + 1, DEPTH:top, lanes : 2 * lanes] = plane
 
         unpack(got_a[0, j], got_a[1, j], put_a)
-
-    def section_coefs(z, carry):
-        for j in range(2):
-            coef_a[j, z] = ext_a[2, z] * (1.0 + 0.5 * jnp.tanh(ext_a[j, z]))
-        return carry
-
-    lax.fori_loop(0, depth_z + 2, section_coefs, 0)
 
     q_own = [[pick(q_table[m][j], q_table[2 + m][2 + j]) for j in range(2)] for m in range(2)]
     q_far = [[pick(q_table[2 + m][j], q_table[m][2 + j]) for j in range(2)] for m in range(2)]
@@ -363,35 +398,42 @@
     def middle(plane):
         return plane[DEPTH:top, 0:lanes]
 
-    def fluxes(z, carry):
+    def fluxes(z):
         flux, increment = [], []
         for j in range(2):
-            cells, coefs = ext_a[j, z + 1], coef_a[j, z + 1]
+            cells, coefs = ext_a[j, z + 1], ext_a[2 + j, z + 1]
             here, coef_here = middle(cells), middle(coefs)
             total = jnp.zeros_like(here)
             for member in range(4):
                 face = 0.5 * (coef_here + middle(near(coefs, member)))
                 total = total + face * (middle(near(cells, member)) - here)
             for level in (z, z + 2):
-                face = 0.5 * (coef_here + middle(coef_a[j, level]))
+                face = 0.5 * (coef_here + middle(ext_a[2 + j, level]))
                 total = total + face * (middle(ext_a[j, level]) - here)
             flux.append(total + react_ref[z] * here * (1.0 - here * here))
             increment.append(here - prev_ref[z])
-        for m in range(2):
-            part[m, z] = (
-                q_own[m][0] * flux[0] + q_own[m][1] * flux[1]
-                - c_own[m][0] * increment[0] - c_own[m][1] * increment[1]
-            )
-            part_out[m, z] = (
-                q_far[m][0] * flux[0] + q_far[m][1] * flux[1]
-                - c_far[m][0] * increment[0] - c_far[m][1] * increment[1]
-            )
-        return carry
+        near_part = [
+            q_own[m][0] * flux[0] + q_own[m][1] * flux[1]
+            - c_own[m][0] * increment[0] - c_own[m][1] * increment[1]
+            for m in range(2)
+        ]
+        far_part = [
+            q_far[m][0] * flux[0] + q_far[m][1] * flux[1]
+            - c_far[m][0] * increment[0] - c_far[m][1] * increment[1]
+            for m in range(2)
+        ]
+
+        def store():
+            for m in range(2):
+                part[m, z] = near_part[m]
+                part_out[m, z] = far_part[m]
+
+        return store
 
     chunk = depth_z // 4
     swap = []
     for at in range(4):
-        lax.fori_loop(at * chunk, (at + 1) * chunk, fluxes, 0)
+        planes(fluxes, at * chunk, (at + 1) * chunk, 2)
         piece = pl.ds(at * chunk, chunk)
         one = copy(part_out.at[:, piece], part_in.at[:, piece], {"section": 1 - half})
         one.start()
@@ -423,46 +465,53 @@
 
     lax.fori_loop(0, depth_z + 1, depth_faces, 0)
 
-    def operator(z, carry):
+    def operator(z):
         coefs = ext_b[0, z + 1]
         diag = real_part - ext_b[1, z + 1] + face_z[z] + face_z[z + 1]
-        for member in range(4):
-            face = 0.5 * (coefs + near(coefs, member))
-            faces[member, z] = face
+        sides = [0.5 * (coefs + near(coefs, member)) for member in range(4)]
+        for face in sides:
             diag = diag + face
         scale = keep / (diag * diag + coupling * coupling)
-        alpha[z] = diag * scale
-        beta[z] = coupling * scale
-        return carry
-
-    lax.fori_loop(0, depth_z, operator, 0)
+
+        def store():
+            for member in range(4):
+                faces[member, z] = sides[member]
+            alpha[z] = diag * scale
+            beta[z] = coupling * scale
+
+        return store
+
+    planes(operator, 0, depth_z, 2)
 
     for m in range(1, DEPTH):
         for field in range(2):
-            hist[m, field, 0] = jnp.zeros((wide, 2 * lanes), jnp.float32)
-            hist[m, field, depth_z + 1] = jnp.zeros((wide, 2 * lanes), jnp.float32)
+            hist[m][field, 0] = jnp.zeros((wide, 2 * lanes), jnp.float32)
+            hist[m][field, depth_z + 1] = jnp.zeros((wide, 2 * lanes), jnp.float32)
 
     for one in swap:
         one.wait_recv()
 
-    def first_scaled(z, carry):
+    def first_scaled(z):
         rhs = [part[m, z] + part_in[m, z] for m in range(2)]
         a, b = middle(alpha[z]), middle(beta[z])
-        for m in range(2):
-            basis[0, m, z] = rhs[m]
-        hist[0, 0, z + 1, DEPTH:top, 0:lanes] = a * rhs[0] - b * rhs[1]
-        hist[0, 1, z + 1, DEPTH:top, 0:lanes] = b * rhs[0] + a * rhs[1]
-        return carry
-
-    lax.fori_loop(0, depth_z, first_scaled, 0)
+
+        def store():
+            for m in range(2):
+                basis[0, m, z] = rhs[m]
+            hist[0][0, z + 1, DEPTH:top, 0:lanes] = a * rhs[0] - b * rhs[1]
+            hist[0][1, z + 1, DEPTH:top, 0:lanes] = b * rhs[0] + a * rhs[1]
+
+        return store
+
+    planes(first_scaled, 0, depth_z, 4)
     copies_c = slabs(
-        hist.at[0, :, body_z, pl.ds(DEPTH, DEPTH), own],
-        hist.at[0, :, body_z, pl.ds(top - DEPTH, DEPTH), own],
-        lambda where: hist.at[0, :, body_z, where, own],
+        hist[0].at[:, body_z, pl.ds(DEPTH, DEPTH), own],
+        hist[0].at[:, body_z, pl.ds(top - DEPTH, DEPTH), own],
+        lambda where: hist[0].at[:, body_z, where, own],
     )
     start(copies_c)
     for j in range(2):
-        pack(lambda z: hist[0, j, z + 1, DEPTH:top, 0:lanes], pack_c.at[0, j], pack_c.at[1, j])
+        pack(lambda z: hist[0][j, z + 1, DEPTH:top, 0:lanes], pack_c.at[0, j], pack_c.at[1, j])
     more_c = strips(pack_c, got_c, True)
     start(more_c)
     copies_c = copies_c + more_c
@@ -470,37 +519,40 @@
 
     for j in range(2):
         def put_c(z, plane):
-            hist[0, j, z + 1, :, lanes : 2 * lanes] = plane
+            hist[0][j, z + 1, :, lanes : 2 * lanes] = plane
 
         unpack(got_c[0, j], got_c[1, j], put_c)
 
     for m in range(DEPTH - 1):
-        def apply(z, carry):
+        def apply(z):
             around = []
             for field in range(2):
-                cells = hist[m, field, z + 1]
-                total = face_z[z] * hist[m, field, z] + face_z[z + 1] * hist[m, field, z + 2]
+                cells = hist[m][field, z + 1]
+                total = face_z[z] * hist[m][field, z] + face_z[z + 1] * hist[m][field, z + 2]
                 for member in range(4):
                     total = total + faces[member, z] * near(cells, member)
                 around.append(total)
-            if m % 2 == 1:
+            a, b = alpha[z], beta[z]
+            scaled = [a * around[0] - b * around[1], b * around[0] + a * around[1]]
+
+            def store():
                 for field in range(2):
-                    basis[(m + 1) // 2, field, z] = middle(around[field])
-            a, b = alpha[z], beta[z]
-            hist[m + 1, 0, z + 1] = a * around[0] - b * around[1]
-            hist[m + 1, 1, z + 1] = b * around[0] + a * around[1]
-            return carry
-
-        lax.fori_loop(0, depth_z, apply, 0)
+                    if m % 2 == 1:
+                        basis[(m + 1) // 2, field, z] = middle(around[field])
+                    hist[m + 1][field, z + 1] = scaled[field]
+
+            return store
+
+        planes(apply, 0, depth_z, 2)
 
     index = [(i, j) for i in range(ITERS + 1) for j in range(i, ITERS + 1)]
 
     def last_apply(z, carry):
         totals = list(carry)
         for field in range(2):
-            cells = hist[DEPTH - 1, field, z + 1]
-            total = middle(face_z[z]) * middle(hist[DEPTH - 1, field, z])
-            total = total + middle(face_z[z + 1]) * middle(hist[DEPTH - 1, field, z + 2])
+            cells = hist[DEPTH - 1][field, z + 1]
+            total = middle(face_z[z]) * middle(hist[DEPTH - 1][field, z])
+            total = total + middle(face_z[z + 1]) * middle(hist[DEPTH - 1][field, z + 2])
             for member in range(4):
                 total = total + middle(faces[member, z]) * middle(near(cells, member))
             members_of = [basis[k, field, z] for k in range(ITERS)] + [total]
@@ -512,9 +564,16 @@
 
     zeros = tuple(jnp.zeros((8, lanes), jnp.float32) for pair in index)
     sums = lax.fori_loop(0, depth_z, last_apply, zeros)
-    gram[0, len(index) : 16] = jnp.zeros((16 - len(index), lanes), jnp.float32)
-    for at, total in enumerate(sums):
-        gram[0, at : at + 1] = jnp.sum(total, axis=0, keepdims=True)
+    square = jnp.concatenate(
+        [jnp.sum(total, axis=0, keepdims=True) for total in sums]
+        + [jnp.zeros((16 - len(index), lanes), jnp.float32)],
+        axis=0,
+    )
+    diagonal = lax.broadcasted_iota(jnp.int32, (16, lanes), 0) == lax.broadcasted_iota(
+        jnp.int32, (16, lanes), 1
+    )
+    square = jnp.where(diagonal, jnp.sum(square, axis=1, keepdims=True), 0.0)
+    gram[0] = jnp.sum(square, axis=0, keepdims=True)
 
     def gram_copy(offset):
         return pltpu.make_async_remote_copy(
@@ -545,11 +604,11 @@
     for one in swap:
         one.wait_send()
     lax.fori_loop(1, members, gram_take, 0)
-    table = gram[0]
     turn = [lax.rem(me - place + members, members) for place in range(members)]
     table = gram[turn[0]]
     for place in range(1, members):
         table = table + gram[turn[place]]
+    table = jnp.where(diagonal, jnp.broadcast_to(table, (16, lanes)), 0.0)
     table = jnp.sum(table, axis=1, keepdims=True)
     entry = {}
     for at, (i, j) in enumerate(index):
@@ -582,22 +641,25 @@
     p_far = [[pick(p_table[2 + j][m], p_table[j][2 + m]) for m in range(2)] for j in range(2)]
     gain_at = [jnp.broadcast_to(gains[k], (rows, lanes)) for k in range(ITERS)]
 
-    def correct(z, carry):
+    def correct(z):
         fix = []
         for field in range(2):
             total = None
             for k in range(ITERS):
-                search = middle(hist[2 * k, field, z + 1]) + middle(hist[2 * k + 1, field, z + 1])
+                search = middle(hist[2 * k][field, z + 1]) + middle(hist[2 * k + 1][field, z + 1])
                 total = gain_at[k] * search if total is None else total + gain_at[k] * search
             fix.append(total)
-        for j in range(2):
-            corr_out[j, z] = p_far[j][0] * fix[0] + p_far[j][1] * fix[1]
-            part[j, z] = sec_ref[j, z] + p_own[j][0] * fix[0] + p_own[j][1] * fix[1]
-        return carry
+
+        def store():
+            for j in range(2):
+                corr_out[j, z] = p_far[j][0] * fix[0] + p_far[j][1] * fix[1]
+                part[j, z] = sec_ref[j, z] + p_own[j][0] * fix[0] + p_own[j][1] * fix[1]
+
+        return store
 
     final = []
     for at in range(4):
-        lax.fori_loop(at * chunk, (at + 1) * chunk, correct, 0)
+        planes(correct, at * chunk, (at + 1) * chunk, 4)
         piece = pl.ds(at * chunk, chunk)
         one = copy(corr_out.at[:, piece], corr_in.at[:, piece], {"section": 1 - half})
         one.start()
@@ -605,12 +667,8 @@
     for at in range(4):
         final[at].wait_recv()
 
-        def finish(z, carry):
-            for j in range(2):
-                out_ref[j, z] = part[j, z] + corr_in[j, z]
-            return carry
-
-        lax.fori_loop(at * chunk, (at + 1) * chunk, finish, 0)
+        piece = pl.ds(at * chunk, chunk)
+        out_ref[:, piece] = part[:, piece] + corr_in[:, piece]
     for one in final:
         one.wait_send()
     lax.fori_loop(1, members, gram_release, 0)
@@ -635,30 +693,34 @@
         return pl.pallas_call(
             functools.partial(kernel, sx_count, sy_count, tables),
             out_shape=jax.ShapeDtypeStruct(sections.shape, f32),
-            in_specs=[pl.BlockSpec(memory_space=pltpu.VMEM)] * 4,
+            in_specs=[pl.BlockSpec(memory_space=pl.ANY)] * 4,
             out_specs=pl.BlockSpec(memory_space=pltpu.VMEM),
             scratch_shapes=[
-                vmem((3,) + ext, f32),
-                vmem((2,) + ext, f32),
+                vmem((depth_z, rows, lanes), f32),
+                vmem(block, f32),
+                vmem((depth_z, rows, lanes), f32),
+                vmem((depth_z, rows, lanes), f32),
+                vmem((4,) + ext, f32),
                 vmem((2,) + ext, f32),
                 vmem((4,) + flat, f32),
                 vmem((depth_z + 1, wide, 2 * lanes), f32),
                 vmem(flat, f32),
                 vmem(flat, f32),
-                vmem((DEPTH, 2) + ext, f32),
+                *[vmem((2,) + ext, f32) for m in range(DEPTH)],
                 vmem((ITERS,) + block, f32),
                 vmem(block, f32),
                 vmem(block, f32),
                 vmem(block, f32),
                 vmem(block, f32),
                 vmem(block, f32),
-                vmem((2, 3, rows, lanes), f32),
-                vmem((2, 3, rows, lanes), f32),
+                vmem((2, 4, rows, lanes), f32),
+                vmem((2, 4, rows, lanes), f32),
                 vmem((2, 2, rows, lanes), f32),
                 vmem((2, 2, wide, lanes), f32),
                 vmem((2, 2, rows, lanes), f32),
                 vmem((2, 2, wide, lanes), f32),
-                vmem((members, 16, lanes), f32),
+                vmem((members, 1, lanes), f32),
+                pltpu.SemaphoreType.DMA((4,)),
                 pltpu.SemaphoreType.DMA((32,)),
                 pltpu.SemaphoreType.DMA((32,)),
                 pltpu.SemaphoreType.DMA((members,)),

time: 53.9 us -> 47.9 us (0.89)
  Pallas kernels: 49.4 us -> 43.3 us
    pallas_call x1, Pallas kernels: 49.4 us -> 43.3 us  [body(): pl.pallas_call(functools.partial(kernel, sx_count, sy_count, tables), out...]
where the time goes in v2:
time: 47.9 us; the launch traced here: 47.7 us
  Pallas kernels  43.3 us (90%)
  local copies, waits for them, and re-layouts  4.37 us (9%)
    pallas_call x1, Pallas kernels, body(): pl.pallas_call(functools.partial(kernel, sx_count, sy_count, tables), out...  43.3 us
    unnamed x9, local copies, waits for them, and re-layouts  4.37 us

profile of v2, /device:TPU:0, one launch (start us, length us, event | category | flops | bytes accessed | tf_op | source)
XLA Modules:
  0.0 47.7 jit_solution(9516657071293122816)
XLA Ops:
  0.0 0.0 copy-start
  0.0 0.9 %copy-done = f32[2,16,16,128]{3,2,1,0:T(8,128)S(1)} copy-done((f32[2,16,16,128]{3,2,1,0:T(8,128)S(1)}, f32[2,16,16,128]{3,2,1,0:T(8,128)}, u32[]{:S(2)}) %copy-start) | copy-done | bytes 262168
  1.0 0.0 copy-start.1
  1.0 0.9 %copy-done.1 = f32[16,16,128]{2,1,0:T(8,128)S(1)} copy-done((f32[16,16,128]{2,1,0:T(8,128)S(1)}, f32[16,16,128]{2,1,0:T(8,128)}, u32[]{:S(2)}) %copy-start.1) | copy-done | bytes 131096
  1.9 0.0 copy-start.2
  1.9 0.9 %copy-done.2 = f32[16,16,128]{2,1,0:T(8,128)S(1)} copy-done((f32[16,16,128]{2,1,0:T(8,128)S(1)}, f32[16,16,128]{2,1,0:T(8,128)}, u32[]{:S(2)}) %copy-start.2) | copy-done | bytes 131096
  2.8 0.0 copy-start.3
  2.8 0.9 %copy-done.3 = f32[16,16,128]{2,1,0:T(8,128)S(1)} copy-done((f32[16,16,128]{2,1,0:T(8,128)S(1)}, f32[16,16,128]{2,1,0:T(8,128)}, u32[]{:S(2)}) %copy-start.3) | copy-done | bytes 131096
  3.7 43.3 %shard_map.46 = f32[2,16,16,128]{3,2,1,0:T(8,128)S(1)} custom-call(f32[16,16,128]{2,1,0:T(8,128)S(1)} %copy-done.1, f32[2,16,16,128]{3,2,1,0:T(8,128)S(1)} %copy-done, f32[16,16,128]{2,1,0:T(8,128)S(1)} %copy-done.2, f32[16,16,128]{2,1,0:T(8,128)S(1)} %copy-done.3), custom_call_target="tpu_custom_call" | custom-call | tf_op jit(solution)/shard_map/pallas_call | solution.py:693
  47.0 0.7 %copy.6 = f32[2,16,16,128]{3,2,1,0:T(8,128)} copy(f32[2,16,16,128]{3,2,1,0:T(8,128)S(1)} %shard_map.46) | data formatting | bytes 524288
Async XLA Ops:
  0.0 0.9 %copy-start = (f32[2,16,16,128]{3,2,1,0:T(8,128)S(1)}, f32[2,16,16,128]{3,2,1,0:T(8,128)}, u32[]{:S(2)}) copy-start(f32[2,16,16,128]{3,2,1,0:T(8,128)} %sec_any.1) | copy-start | bytes 786436
  1.0 0.9 %copy-start.1 = (f32[16,16,128]{2,1,0:T(8,128)S(1)}, f32[16,16,128]{2,1,0:T(8,128)}, u32[]{:S(2)}) copy-start(f32[16,16,128]{2,1,0:T(8,128)} %prev_any.1) | copy-start | bytes 393220
  1.9 0.9 %copy-start.2 = (f32[16,16,128]{2,1,0:T(8,128)S(1)}, f32[16,16,128]{2,1,0:T(8,128)}, u32[]{:S(2)}) copy-start(f32[16,16,128]{2,1,0:T(8,128)} %diff_any.1) | copy-start | bytes 393220
  2.8 0.9 %copy-start.3 = (f32[16,16,128]{2,1,0:T(8,128)S(1)}, f32[16,16,128]{2,1,0:T(8,128)}, u32[]{:S(2)}) copy-start(f32[16,16,128]{2,1,0:T(8,128)} %react_any.1) | copy-start | bytes 393220

commit v3 on v2

--- a/solution.py
+++ b/solution.py
@@ -169,18 +169,19 @@
     sx_count, sy_count, tables,
     prev_any, sec_any, diff_any, react_any, out_ref,
     prev_ref, sec_ref, diff_ref, react_ref,
-    ext_a, ext_b, faces, face_z, alpha, beta, *rest,
+    ext_a, ext_b, faces, face_x, alpha, beta, *rest,
 ):
     hist, rest = rest[:DEPTH], rest[DEPTH:]
+    powers, rest = rest[: ITERS - 1], rest[ITERS - 1 :]
     (
     basis, part, part_out, part_in, corr_out, corr_in,
     pack_a, got_a, pack_b, got_b, pack_c, got_c, gram, load_sem,
     send_sem, recv_sem, gram_send, gram_recv,
     ) = rest
-    depth_z, rows, lanes = prev_ref.shape
+    depth_z, lanes = ext_a.shape[2], prev_ref.shape[1]
+    rows = prev_ref.shape[0] // depth_z
     top = DEPTH + rows
-    wide = rows + 2 * DEPTH
-    group = lanes // DEPTH
+    group = rows
     sx, sy, half = lax.axis_index("sx"), lax.axis_index("sy"), lax.axis_index("section")
     q_table, c_table, p_table, pairs = tables
 
@@ -218,33 +219,42 @@
     lax.fori_loop(1, members, greet, 0)
     pl.semaphore_signal(barrier, inc=1, device_id={"section": 1 - half}, device_id_type=MESH)
 
-    lane_group = lax.broadcasted_iota(jnp.int32, (rows, lanes), 1) // DEPTH
+    lane_group = lax.broadcasted_iota(jnp.int32, (depth_z, lanes), 1) // DEPTH
 
     def pack(plane_of, low, high):
-        down = jnp.zeros((rows, lanes), jnp.float32)
-        up = jnp.zeros((rows, lanes), jnp.float32)
-        for z in range(depth_z):
-            plane = plane_of(z)
-            if z > 0:
-                plane = pltpu.roll(plane, DEPTH * z, 1)
-            down = jnp.where(lane_group == z, plane, down)
-            up = jnp.where(lane_group == (z + group - 1) % group, plane, up)
+        down = jnp.zeros((depth_z, lanes), jnp.float32)
+        up = jnp.zeros((depth_z, lanes), jnp.float32)
+        for x in range(rows):
+            plane = plane_of(x)
+            if x > 0:
+                plane = pltpu.roll(plane, DEPTH * x, 1)
+            down = jnp.where(lane_group == x, plane, down)
+            up = jnp.where(lane_group == (x + group - 1) % group, plane, up)
         low[...] = down
         high[...] = up
 
-    def unpack(from_high, from_low, store):
-        count = from_high.shape[0]
-        groups = lax.broadcasted_iota(jnp.int32, (count, lanes), 1) // DEPTH
-        zero = jnp.zeros((count, lanes), jnp.float32)
-        for z in range(depth_z):
+    def unpack(from_high, from_low, members_x, store):
+        for x in members_x:
             mixed = jnp.where(
-                groups == z,
+                lane_group == x,
                 from_high,
-                jnp.where(groups == (z + group - 1) % group, from_low, zero),
+                jnp.where(lane_group == (x + group - 1) % group, from_low, 0.0),
             )
-            if z > 0:
-                mixed = pltpu.roll(mixed, lanes - DEPTH * z, 1)
-            store(z, mixed)
+            if x > 0:
+                mixed = pltpu.roll(mixed, lanes - DEPTH * x, 1)
+            store(x, mixed)
+
+    def unpack_wide(got, j, target):
+        for place, members_x in ((0, range(rows - DEPTH, rows)), (1, range(rows)), (2, range(DEPTH))):
+            first = (DEPTH - rows, DEPTH, top)[place]
+
+            def store(x, plane):
+                target[j, first + x, :, lanes : 2 * lanes] = plane
+
+            unpack(got[0, place, j], got[1, place, j], members_x, store)
+
+    def column(ref, x):
+        return ref[pl.ds(x, depth_z, stride=rows), :]
 
     for one in loads:
         one.wait()
@@ -260,27 +270,27 @@
 
         lax.fori_loop(0, (most - least) // batch, several, 0)
 
-    def own_coefs(z):
-        before, diffusivity = prev_ref[z], diff_ref[z]
-        cells = [sec_ref[j, z] for j in range(2)]
+    def own_coefs(x):
+        before, diffusivity = column(prev_ref, x), column(diff_ref, x)
+        cells = [column(sec_ref.at[j], x) for j in range(2)]
         coefs = [diffusivity * (1.0 + 0.5 * jnp.tanh(cells[j])) for j in range(2)]
         coef = diffusivity * (1.0 + 0.5 * jnp.tanh(before))
-        slope = react_ref[z] * (1.0 - 3.0 * before * before)
+        slope = column(react_ref, x) * (1.0 - 3.0 * before * before)
 
         def store():
             for j in range(2):
-                ext_a[j, z + 1, DEPTH:top, 0:lanes] = cells[j]
-                ext_a[2 + j, z + 1, DEPTH:top, 0:lanes] = coefs[j]
-            ext_b[0, z + 1, DEPTH:top, 0:lanes] = coef
-            ext_b[1, z + 1, DEPTH:top, 0:lanes] = slope
+                ext_a[j, x + DEPTH, :, 0:lanes] = cells[j]
+                ext_a[2 + j, x + DEPTH, :, 0:lanes] = coefs[j]
+            ext_b[0, x + DEPTH, :, 0:lanes] = coef
+            ext_b[1, x + DEPTH, :, 0:lanes] = slope
 
         return store
 
-    planes(own_coefs, 0, depth_z, 2)
+    planes(own_coefs, 0, rows, 2)
     for j in range(4):
-        pack(lambda z: ext_a[j, z + 1, DEPTH:top, 0:lanes], pack_a.at[0, j], pack_a.at[1, j])
+        pack(lambda x: ext_a[j, x + DEPTH, :, 0:lanes], pack_a.at[0, j], pack_a.at[1, j])
     for j in range(2):
-        pack(lambda z: ext_b[j, z + 1, DEPTH:top, 0:lanes], pack_b.at[0, j], pack_b.at[1, j])
+        pack(lambda x: ext_b[j, x + DEPTH, :, 0:lanes], pack_b.at[0, j], pack_b.at[1, j])
 
     pl.semaphore_wait(barrier, members)
 
@@ -298,11 +308,11 @@
             device_id_type=MESH,
         )
 
+    wide = rows + 2 * DEPTH
     left, right = lax.rem(sx + sx_count - 1, sx_count), lax.rem(sx + 1, sx_count)
     below, above = lax.rem(sy + sy_count - 1, sy_count), lax.rem(sy + 1, sy_count)
     has_left, has_right = sx > 0, sx < sx_count - 1
     has_below, has_above = sy > 0, sy < sy_count - 1
-    body_z = pl.ds(1, depth_z)
     own = pl.ds(0, lanes)
     low_rows, high_rows = pl.ds(0, DEPTH), pl.ds(top, DEPTH)
 
@@ -318,15 +328,15 @@
             (0, below, has_below, has_above),
             (1, above, has_above, has_below),
         ):
-            middle = got.at[side, :, pl.ds(DEPTH, rows), :] if corners else got.at[side]
+            middle = got.at[side, 1] if corners else got.at[side]
             result.append((out_ok, in_ok, copy(packed.at[side], middle, {"sy": device})))
             if corners:
                 result.append((
                     out_ok & has_left,
                     in_ok & has_right,
                     copy(
-                        packed.at[side, :, pl.ds(0, DEPTH), :],
-                        got.at[side, :, high_rows, :],
+                        packed.at[side],
+                        got.at[side, 2],
                         {"sx": left, "sy": device},
                     ),
                 ))
@@ -334,8 +344,8 @@
                     out_ok & has_right,
                     in_ok & has_left,
                     copy(
-                        packed.at[side, :, pl.ds(rows - DEPTH, DEPTH), :],
-                        got.at[side, :, low_rows, :],
+                        packed.at[side],
+                        got.at[side, 0],
                         {"sx": right, "sy": device},
                     ),
                 ))
@@ -359,8 +369,8 @@
         has_left,
         has_right,
         copy(
-            ext_a.at[:, body_z, pl.ds(DEPTH, 1), own],
-            ext_a.at[:, body_z, edge[0], own],
+            ext_a.at[:, pl.ds(DEPTH, 1), :, own],
+            ext_a.at[:, edge[0], :, own],
             {"sx": left},
         ),
     ))
@@ -368,27 +378,27 @@
         has_right,
         has_left,
         copy(
-            ext_a.at[:, body_z, pl.ds(top - 1, 1), own],
-            ext_a.at[:, body_z, edge[1], own],
+            ext_a.at[:, pl.ds(top - 1, 1), :, own],
+            ext_a.at[:, edge[1], :, own],
             {"sx": right},
         ),
     ))
     start(copies_a)
     copies_b = strips(pack_b, got_b, True)
     copies_b += slabs(
-        ext_b.at[:, body_z, pl.ds(DEPTH, DEPTH), own],
-        ext_b.at[:, body_z, pl.ds(top - DEPTH, DEPTH), own],
-        lambda where: ext_b.at[:, body_z, where, own],
+        ext_b.at[:, pl.ds(DEPTH, DEPTH), :, own],
+        ext_b.at[:, pl.ds(top - DEPTH, DEPTH), :, own],
+        lambda where: ext_b.at[:, where, :, own],
     )
     start(copies_b)
 
     receive(copies_a)
 
     for j in range(4):
-        def put_a(z, plane):
-            ext_a[j, z + 1, DEPTH:top, lanes : 2 * lanes] = plane
-
-        unpack(got_a[0, j], got_a[1, j], put_a)
+        def put_a(x, plane):
+            ext_a[j, x + DEPTH, :, lanes : 2 * lanes] = plane
+
+        unpack(got_a[0, j], got_a[1, j], range(rows), put_a)
 
     q_own = [[pick(q_table[m][j], q_table[2 + m][2 + j]) for j in range(2)] for m in range(2)]
     q_far = [[pick(q_table[2 + m][j], q_table[m][2 + j]) for j in range(2)] for m in range(2)]
@@ -396,22 +406,32 @@
     c_far = [[pick(c_table[2 + m][j], c_table[m][2 + j]) for j in range(2)] for m in range(2)]
 
     def middle(plane):
-        return plane[DEPTH:top, 0:lanes]
-
-    def fluxes(z):
+        return plane[:, 0:lanes]
+
+    z_at = lax.broadcasted_iota(jnp.int32, (depth_z, 2 * lanes), 0)
+    has_next = (z_at < depth_z - 1, z_at > 0)
+
+    def around_z(plane, member):
+        mask = has_next[member][:, 0 : plane.shape[1]]
+        return jnp.where(mask, near(plane, member), 0.0)
+
+    def fluxes(x):
         flux, increment = [], []
         for j in range(2):
-            cells, coefs = ext_a[j, z + 1], ext_a[2 + j, z + 1]
+            cells, coefs = ext_a[j, x + DEPTH], ext_a[2 + j, x + DEPTH]
             here, coef_here = middle(cells), middle(coefs)
             total = jnp.zeros_like(here)
-            for member in range(4):
+            for member in range(2):
+                face = 0.5 * (coef_here + around_z(coef_here, member))
+                total = total + face * (around_z(here, member) - here)
+            for member in (2, 3):
                 face = 0.5 * (coef_here + middle(near(coefs, member)))
                 total = total + face * (middle(near(cells, member)) - here)
-            for level in (z, z + 2):
-                face = 0.5 * (coef_here + middle(ext_a[2 + j, level]))
-                total = total + face * (middle(ext_a[j, level]) - here)
-            flux.append(total + react_ref[z] * here * (1.0 - here * here))
-            increment.append(here - prev_ref[z])
+            for place in (x + DEPTH - 1, x + DEPTH + 1):
+                face = 0.5 * (coef_here + ext_a[2 + j, place, :, 0:lanes])
+                total = total + face * (ext_a[j, place, :, 0:lanes] - here)
+            flux.append(total + column(react_ref, x) * here * (1.0 - here * here))
+            increment.append(here - column(prev_ref, x))
         near_part = [
             q_own[m][0] * flux[0] + q_own[m][1] * flux[1]
             - c_own[m][0] * increment[0] - c_own[m][1] * increment[1]
@@ -425,12 +445,12 @@
 
         def store():
             for m in range(2):
-                part[m, z] = near_part[m]
-                part_out[m, z] = far_part[m]
+                part[m, x] = near_part[m]
+                part_out[m, x] = far_part[m]
 
         return store
 
-    chunk = depth_z // 4
+    chunk = rows // 4
     swap = []
     for at in range(4):
         planes(fluxes, at * chunk, (at + 1) * chunk, 2)
@@ -442,128 +462,132 @@
     receive(copies_b)
 
     for j in range(2):
-        def put_b(z, plane):
-            ext_b[j, z + 1, :, lanes : 2 * lanes] = plane
-
-        unpack(got_b[0, j], got_b[1, j], put_b)
+        unpack_wide(got_b, j, ext_b)
 
     real_part = pick(pairs[0][0] / step_size, pairs[1][0] / step_size)
     coupling = pick(pairs[0][1] / step_size, pairs[1][1] / step_size)
-    row_at = lax.broadcasted_iota(jnp.int32, (wide, 2 * lanes), 0)
-    lane_at = lax.broadcasted_iota(jnp.int32, (wide, 2 * lanes), 1)
-    inside = ((row_at >= DEPTH) | has_left) & ((row_at < top) | has_right)
-    inside = inside & (
+    lane_at = lax.broadcasted_iota(jnp.int32, (depth_z, 2 * lanes), 1)
+    inside = (
         (lane_at < lanes)
         | ((lane_at < lanes + DEPTH) & has_above)
         | ((lane_at >= 2 * lanes - DEPTH) & has_below)
     )
     keep = inside.astype(jnp.float32)
 
-    def depth_faces(z, carry):
-        face_z[z] = 0.5 * (ext_b[0, z] + ext_b[0, z + 1])
-        return carry
-
-    lax.fori_loop(0, depth_z + 1, depth_faces, 0)
-
-    def operator(z):
-        coefs = ext_b[0, z + 1]
-        diag = real_part - ext_b[1, z + 1] + face_z[z] + face_z[z + 1]
-        sides = [0.5 * (coefs + near(coefs, member)) for member in range(4)]
-        for face in sides:
+    def x_faces(x):
+        face = 0.5 * (ext_b[0, x] + ext_b[0, x + 1])
+
+        def store():
+            face_x[x] = face
+
+        return store
+
+    planes(x_faces, 0, wide - 1, 1)
+
+    def operator(x):
+        coefs = ext_b[0, x]
+        diag = real_part - ext_b[1, x] + face_x[x - 1] + face_x[x]
+        sides = []
+        for member in range(2):
+            face = 0.5 * (coefs + around_z(coefs, member))
             diag = diag + face
+            sides.append(jnp.where(has_next[member], face, 0.0))
+        for member in (2, 3):
+            face = 0.5 * (coefs + near(coefs, member))
+            diag = diag + face
+            sides.append(face)
+        inside_x = ((x >= DEPTH) | has_left) & ((x < top) | has_right)
         scale = keep / (diag * diag + coupling * coupling)
+        scale = jnp.where(inside_x, scale, 0.0)
 
         def store():
             for member in range(4):
-                faces[member, z] = sides[member]
-            alpha[z] = diag * scale
-            beta[z] = coupling * scale
+                faces[member, x] = sides[member]
+            alpha[x] = diag * scale
+            beta[x] = coupling * scale
 
         return store
 
-    planes(operator, 0, depth_z, 2)
-
-    for m in range(1, DEPTH):
-        for field in range(2):
-            hist[m][field, 0] = jnp.zeros((wide, 2 * lanes), jnp.float32)
-            hist[m][field, depth_z + 1] = jnp.zeros((wide, 2 * lanes), jnp.float32)
-
-    for one in swap:
-        one.wait_recv()
-
-    def first_scaled(z):
-        rhs = [part[m, z] + part_in[m, z] for m in range(2)]
-        a, b = middle(alpha[z]), middle(beta[z])
+    planes(operator, 1, wide - 1, 2)
+
+    def first_scaled(x):
+        rhs = [part[m, x] + part_in[m, x] for m in range(2)]
+        a, b = middle(alpha[x + DEPTH]), middle(beta[x + DEPTH])
 
         def store():
             for m in range(2):
-                basis[0, m, z] = rhs[m]
-            hist[0][0, z + 1, DEPTH:top, 0:lanes] = a * rhs[0] - b * rhs[1]
-            hist[0][1, z + 1, DEPTH:top, 0:lanes] = b * rhs[0] + a * rhs[1]
+                basis[0, m, x] = rhs[m]
+            hist[0][0, x + DEPTH, :, 0:lanes] = a * rhs[0] - b * rhs[1]
+            hist[0][1, x + DEPTH, :, 0:lanes] = b * rhs[0] + a * rhs[1]
 
         return store
 
-    planes(first_scaled, 0, depth_z, 4)
     copies_c = slabs(
-        hist[0].at[:, body_z, pl.ds(DEPTH, DEPTH), own],
-        hist[0].at[:, body_z, pl.ds(top - DEPTH, DEPTH), own],
-        lambda where: hist[0].at[:, body_z, where, own],
+        hist[0].at[:, pl.ds(DEPTH, DEPTH), :, own],
+        hist[0].at[:, pl.ds(top - DEPTH, DEPTH), :, own],
+        lambda where: hist[0].at[:, where, :, own],
     )
-    start(copies_c)
+    for at in range(4):
+        swap[at].wait_recv()
+        planes(first_scaled, at * chunk, (at + 1) * chunk, chunk)
+        if (at + 1) * chunk == DEPTH:
+            start(copies_c[0:1])
+        if (at + 1) * chunk == rows:
+            start(copies_c[1:2])
     for j in range(2):
-        pack(lambda z: hist[0][j, z + 1, DEPTH:top, 0:lanes], pack_c.at[0, j], pack_c.at[1, j])
+        pack(lambda x: hist[0][j, x + DEPTH, :, 0:lanes], pack_c.at[0, j], pack_c.at[1, j])
     more_c = strips(pack_c, got_c, True)
     start(more_c)
     copies_c = copies_c + more_c
     receive(copies_c)
-
     for j in range(2):
-        def put_c(z, plane):
-            hist[0][j, z + 1, :, lanes : 2 * lanes] = plane
-
-        unpack(got_c[0, j], got_c[1, j], put_c)
+        unpack_wide(got_c, j, hist[0])
 
     for m in range(DEPTH - 1):
-        def apply(z):
+        def apply(x):
             around = []
             for field in range(2):
-                cells = hist[m][field, z + 1]
-                total = face_z[z] * hist[m][field, z] + face_z[z + 1] * hist[m][field, z + 2]
+                cells = hist[m][field, x]
+                total = face_x[x - 1] * hist[m][field, x - 1] + face_x[x] * hist[m][field, x + 1]
                 for member in range(4):
-                    total = total + faces[member, z] * near(cells, member)
+                    total = total + faces[member, x] * near(cells, member)
                 around.append(total)
-            a, b = alpha[z], beta[z]
+            a, b = alpha[x], beta[x]
             scaled = [a * around[0] - b * around[1], b * around[0] + a * around[1]]
 
             def store():
                 for field in range(2):
                     if m % 2 == 1:
-                        basis[(m + 1) // 2, field, z] = middle(around[field])
-                    hist[m + 1][field, z + 1] = scaled[field]
+                        powers[(m - 1) // 2][field, x] = middle(around[field])
+                    hist[m + 1][field, x] = scaled[field]
 
             return store
 
-        planes(apply, 0, depth_z, 2)
+        planes(apply, m + 1, wide - 1 - m, 2)
 
     index = [(i, j) for i in range(ITERS + 1) for j in range(i, ITERS + 1)]
 
-    def last_apply(z, carry):
+    def last_apply(x, carry):
         totals = list(carry)
         for field in range(2):
-            cells = hist[DEPTH - 1][field, z + 1]
-            total = middle(face_z[z]) * middle(hist[DEPTH - 1][field, z])
-            total = total + middle(face_z[z + 1]) * middle(hist[DEPTH - 1][field, z + 2])
-            for member in range(4):
-                total = total + middle(faces[member, z]) * middle(near(cells, member))
-            members_of = [basis[k, field, z] for k in range(ITERS)] + [total]
+            at_x = x + DEPTH
+            cells = hist[DEPTH - 1][field, at_x]
+            total = middle(face_x[at_x - 1]) * hist[DEPTH - 1][field, at_x - 1, :, 0:lanes]
+            total = total + middle(face_x[at_x]) * hist[DEPTH - 1][field, at_x + 1, :, 0:lanes]
+            for member in range(2):
+                total = total + middle(faces[member, at_x]) * near(middle(cells), member)
+            for member in (2, 3):
+                total = total + middle(faces[member, at_x]) * middle(near(cells, member))
+            members_of = [basis[0, field, x]]
+            members_of += [powers[k][field, at_x] for k in range(ITERS - 1)] + [total]
             for at, (i, j) in enumerate(index):
                 product = members_of[i] * members_of[j]
-                for r in range(0, rows, 8):
+                for r in range(0, depth_z, 8):
                     totals[at] = totals[at] + product[r : r + 8]
         return tuple(totals)
 
     zeros = tuple(jnp.zeros((8, lanes), jnp.float32) for pair in index)
-    sums = lax.fori_loop(0, depth_z, last_apply, zeros)
+    sums = lax.fori_loop(0, rows, last_apply, zeros)
     square = jnp.concatenate(
         [jnp.sum(total, axis=0, keepdims=True) for total in sums]
         + [jnp.zeros((16 - len(index), lanes), jnp.float32)],
@@ -639,21 +663,25 @@
 
     p_own = [[pick(p_table[j][m], p_table[2 + j][2 + m]) for m in range(2)] for j in range(2)]
     p_far = [[pick(p_table[2 + j][m], p_table[j][2 + m]) for m in range(2)] for j in range(2)]
-    gain_at = [jnp.broadcast_to(gains[k], (rows, lanes)) for k in range(ITERS)]
-
-    def correct(z):
+    gain_at = [jnp.broadcast_to(gains[k], (depth_z, lanes)) for k in range(ITERS)]
+
+    def correct(x):
         fix = []
         for field in range(2):
             total = None
             for k in range(ITERS):
-                search = middle(hist[2 * k][field, z + 1]) + middle(hist[2 * k + 1][field, z + 1])
+                search = (
+                    hist[2 * k][field, x + DEPTH, :, 0:lanes]
+                    + hist[2 * k + 1][field, x + DEPTH, :, 0:lanes]
+                )
                 total = gain_at[k] * search if total is None else total + gain_at[k] * search
             fix.append(total)
+        base = [ext_a[j, x + DEPTH, :, 0:lanes] for j in range(2)]
 
         def store():
             for j in range(2):
-                corr_out[j, z] = p_far[j][0] * fix[0] + p_far[j][1] * fix[1]
-                part[j, z] = sec_ref[j, z] + p_own[j][0] * fix[0] + p_own[j][1] * fix[1]
+                corr_out[j, x] = p_far[j][0] * fix[0] + p_far[j][1] * fix[1]
+                part[j, x] = base[j] + p_own[j][0] * fix[0] + p_own[j][1] * fix[1]
 
         return store
 
@@ -667,8 +695,9 @@
     for at in range(4):
         final[at].wait_recv()
 
-        piece = pl.ds(at * chunk, chunk)
-        out_ref[:, piece] = part[:, piece] + corr_in[:, piece]
+        for x in range(at * chunk, (at + 1) * chunk):
+            for j in range(2):
+                out_ref[j, pl.ds(x, depth_z, stride=rows), :] = part[j, x] + corr_in[j, x]
     for one in final:
         one.wait_send()
     lax.fori_loop(1, members, gram_release, 0)
@@ -686,39 +715,40 @@
         wide = rows + 2 * DEPTH
         f32 = jnp.float32
         vmem = pltpu.VMEM
-        ext = (depth_z + 2, wide, 2 * lanes)
-        flat = (depth_z, wide, 2 * lanes)
-        block = (2, depth_z, rows, lanes)
+        ext = (wide, depth_z, 2 * lanes)
+        block = (2, rows, depth_z, lanes)
+        flat = (depth_z * rows, lanes)
         members = sx_count * sy_count
         return pl.pallas_call(
             functools.partial(kernel, sx_count, sy_count, tables),
-            out_shape=jax.ShapeDtypeStruct(sections.shape, f32),
-            in_specs=[pl.BlockSpec(memory_space=pl.ANY)] * 4,
+            out_shape=jax.ShapeDtypeStruct((2,) + flat, f32),
+            in_specs=[pl.BlockSpec(memory_space=pltpu.HBM)] * 4,
             out_specs=pl.BlockSpec(memory_space=pltpu.VMEM),
             scratch_shapes=[
-                vmem((depth_z, rows, lanes), f32),
-                vmem(block, f32),
-                vmem((depth_z, rows, lanes), f32),
-                vmem((depth_z, rows, lanes), f32),
+                vmem(flat, f32),
+                vmem((2,) + flat, f32),
+                vmem(flat, f32),
+                vmem(flat, f32),
                 vmem((4,) + ext, f32),
                 vmem((2,) + ext, f32),
-                vmem((4,) + flat, f32),
-                vmem((depth_z + 1, wide, 2 * lanes), f32),
-                vmem(flat, f32),
-                vmem(flat, f32),
+                vmem((4,) + ext, f32),
+                vmem(ext, f32),
+                vmem(ext, f32),
+                vmem(ext, f32),
                 *[vmem((2,) + ext, f32) for m in range(DEPTH)],
-                vmem((ITERS,) + block, f32),
+                *[vmem((2, wide, depth_z, lanes), f32) for m in range(ITERS - 1)],
+                vmem((1,) + block, f32),
                 vmem(block, f32),
                 vmem(block, f32),
                 vmem(block, f32),
                 vmem(block, f32),
                 vmem(block, f32),
-                vmem((2, 4, rows, lanes), f32),
-                vmem((2, 4, rows, lanes), f32),
-                vmem((2, 2, rows, lanes), f32),
-                vmem((2, 2, wide, lanes), f32),
-                vmem((2, 2, rows, lanes), f32),
-                vmem((2, 2, wide, lanes), f32),
+                vmem((2, 4, depth_z, lanes), f32),
+                vmem((2, 4, depth_z, lanes), f32),
+                vmem((2, 2, depth_z, lanes), f32),
+                vmem((2, 3, 2, depth_z, lanes), f32),
+                vmem((2, 2, depth_z, lanes), f32),
+                vmem((2, 3, 2, depth_z, lanes), f32),
                 vmem((members, 1, lanes), f32),
                 pltpu.SemaphoreType.DMA((4,)),
                 pltpu.SemaphoreType.DMA((32,)),
@@ -729,7 +759,12 @@
             compiler_params=pltpu.CompilerParams(
                 collective_id=0, has_side_effects=True, vmem_limit_bytes=48 * 1024 * 1024
             ),
-        )(previous, sections, diffusivity, reaction)
+        )(
+            previous.reshape(flat),
+            sections.reshape((2,) + flat),
+            diffusivity.reshape(flat),
+            reaction.reshape(flat),
+        ).reshape(sections.shape)
 
     in_specs = (
         P(None, "sx", "sy"),

time: 47.9 us -> 48.4 us (1.010)
  Pallas kernels: 43.3 us -> 43.8 us
where the time goes in v3:
time: 48.4 us; the launch traced here: 48.2 us
  Pallas kernels  43.8 us (90%)
  local copies, waits for them, and re-layouts  4.37 us (9%)
    pallas_call x1, Pallas kernels, body(): pl.pallas_call(functools.partial(kernel, sx_count, sy_count, tables), out...  43.8 us
    unnamed x9, local copies, waits for them, and re-layouts  4.37 us

profile of v3, /device:TPU:0, one launch (start us, length us, event | category | flops | bytes accessed | tf_op | source)
XLA Modules:
  0.0 48.2 jit_solution(5506657887831653274)
XLA Ops:
  0.0 0.0 copy-start
  0.0 0.9 %copy-done = f32[2,16,16,128]{3,2,1,0:T(8,128)S(1)} copy-done((f32[2,16,16,128]{3,2,1,0:T(8,128)S(1)}, f32[2,16,16,128]{3,2,1,0:T(8,128)}, u32[]{:S(2)}) %copy-start) | copy-done | bytes 262168
  1.0 0.0 copy-start.1
  1.0 0.9 %copy-done.1 = f32[16,16,128]{2,1,0:T(8,128)S(1)} copy-done((f32[16,16,128]{2,1,0:T(8,128)S(1)}, f32[16,16,128]{2,1,0:T(8,128)}, u32[]{:S(2)}) %copy-start.1) | copy-done | bytes 131096
  1.9 0.0 copy-start.2
  1.9 0.9 %copy-done.2 = f32[16,16,128]{2,1,0:T(8,128)S(1)} copy-done((f32[16,16,128]{2,1,0:T(8,128)S(1)}, f32[16,16,128]{2,1,0:T(8,128)}, u32[]{:S(2)}) %copy-start.2) | copy-done | bytes 131096
  2.8 0.0 copy-start.3
  2.8 0.9 %copy-done.3 = f32[16,16,128]{2,1,0:T(8,128)S(1)} copy-done((f32[16,16,128]{2,1,0:T(8,128)S(1)}, f32[16,16,128]{2,1,0:T(8,128)}, u32[]{:S(2)}) %copy-start.3) | copy-done | bytes 131096
  3.7 43.8 %shard_map.46 = f32[2,256,128]{2,1,0:T(8,128)S(1)} custom-call(f32[256,128]{1,0:T(8,128)S(1)} %bitcast.7, f32[2,256,128]{2,1,0:T(8,128)S(1)} %bitcast.6, f32[256,128]{1,0:T(8,128)S(1)} %bitcast.8, f32[256,128]{1,0:T(8,128)S(1)} %bitcast.9), custom_call_target="tpu_custom_call" | custom-call | tf_op jit(solution)/shard_map/pallas_call | solution.py:722
  47.5 0.7 %copy.6 = f32[2,16,16,128]{3,2,1,0:T(8,128)} copy(f32[2,16,16,128]{3,2,1,0:T(8,128)S(1)} %bitcast.5) | data formatting | bytes 524288
Async XLA Ops:
  0.0 0.9 %copy-start = (f32[2,16,16,128]{3,2,1,0:T(8,128)S(1)}, f32[2,16,16,128]{3,2,1,0:T(8,128)}, u32[]{:S(2)}) copy-start(f32[2,16,16,128]{3,2,1,0:T(8,128)} %param.5) | copy-start | bytes 786436
  1.0 0.9 %copy-start.1 = (f32[16,16,128]{2,1,0:T(8,128)S(1)}, f32[16,16,128]{2,1,0:T(8,128)}, u32[]{:S(2)}) copy-start(f32[16,16,128]{2,1,0:T(8,128)} %param.4) | copy-start | bytes 393220
  1.9 0.9 %copy-start.2 = (f32[16,16,128]{2,1,0:T(8,128)S(1)}, f32[16,16,128]{2,1,0:T(8,128)}, u32[]{:S(2)}) copy-start(f32[16,16,128]{2,1,0:T(8,128)} %param.6) | copy-start | bytes 393220
  2.8 0.9 %copy-start.3 = (f32[16,16,128]{2,1,0:T(8,128)S(1)}, f32[16,16,128]{2,1,0:T(8,128)}, u32[]{:S(2)}) copy-start(f32[16,16,128]{2,1,0:T(8,128)} %param.7) | copy-start | bytes 393220

commit v4 on v3

--- a/solution.py
+++ b/solution.py
@@ -260,15 +260,22 @@
         one.wait()
 
     def planes(fn, least, most, batch):
-        def several(at, carry):
-            stores = []
-            for step in range(batch):
-                stores.append(fn(least + at * batch + step))
+        def several(first, count):
+            stores = [fn(first + step) for step in range(count)]
             for store in stores:
                 store()
-            return carry
-
-        lax.fori_loop(0, (most - least) // batch, several, 0)
+
+        full, left_over = (most - least) // batch, (most - least) % batch
+        if full == 1:
+            several(least, batch)
+        else:
+            def turn(at, carry):
+                several(least + at * batch, batch)
+                return carry
+
+            lax.fori_loop(0, full, turn, 0)
+        if left_over:
+            several(most - left_over, left_over)
 
     def own_coefs(x):
         before, diffusivity = column(prev_ref, x), column(diff_ref, x)
@@ -286,7 +293,7 @@
 
         return store
 
-    planes(own_coefs, 0, rows, 2)
+    planes(own_coefs, 0, rows, 4)
     for j in range(4):
         pack(lambda x: ext_a[j, x + DEPTH, :, 0:lanes], pack_a.at[0, j], pack_a.at[1, j])
     for j in range(2):
@@ -453,7 +460,7 @@
     chunk = rows // 4
     swap = []
     for at in range(4):
-        planes(fluxes, at * chunk, (at + 1) * chunk, 2)
+        planes(fluxes, at * chunk, (at + 1) * chunk, chunk)
         piece = pl.ds(at * chunk, chunk)
         one = copy(part_out.at[:, piece], part_in.at[:, piece], {"section": 1 - half})
         one.start()
@@ -482,7 +489,7 @@
 
         return store
 
-    planes(x_faces, 0, wide - 1, 1)
+    planes(x_faces, 0, wide - 1, 4)
 
     def operator(x):
         coefs = ext_b[0, x]
@@ -563,31 +570,37 @@
 
             return store
 
-        planes(apply, m + 1, wide - 1 - m, 2)
+        planes(apply, m + 1, wide - 1 - m, 4)
 
     index = [(i, j) for i in range(ITERS + 1) for j in range(i, ITERS + 1)]
 
-    def last_apply(x, carry):
+    def last_apply(at, carry):
         totals = list(carry)
-        for field in range(2):
-            at_x = x + DEPTH
-            cells = hist[DEPTH - 1][field, at_x]
-            total = middle(face_x[at_x - 1]) * hist[DEPTH - 1][field, at_x - 1, :, 0:lanes]
-            total = total + middle(face_x[at_x]) * hist[DEPTH - 1][field, at_x + 1, :, 0:lanes]
-            for member in range(2):
-                total = total + middle(faces[member, at_x]) * near(middle(cells), member)
-            for member in (2, 3):
-                total = total + middle(faces[member, at_x]) * middle(near(cells, member))
-            members_of = [basis[0, field, x]]
-            members_of += [powers[k][field, at_x] for k in range(ITERS - 1)] + [total]
-            for at, (i, j) in enumerate(index):
-                product = members_of[i] * members_of[j]
-                for r in range(0, depth_z, 8):
-                    totals[at] = totals[at] + product[r : r + 8]
+        ends = {}
+        for step in range(4):
+            at_x = 4 * at + step + DEPTH
+            for field in range(2):
+                cells = hist[DEPTH - 1][field, at_x]
+                total = middle(face_x[at_x - 1]) * hist[DEPTH - 1][field, at_x - 1, :, 0:lanes]
+                total = total + middle(face_x[at_x]) * hist[DEPTH - 1][field, at_x + 1, :, 0:lanes]
+                for member in range(2):
+                    total = total + middle(faces[member, at_x]) * near(middle(cells), member)
+                for member in (2, 3):
+                    total = total + middle(faces[member, at_x]) * middle(near(cells, member))
+                ends[step, field] = total
+        for step in range(4):
+            for field in range(2):
+                members_of = [basis[0, field, 4 * at + step]]
+                members_of += [powers[k][field, 4 * at + step + DEPTH] for k in range(ITERS - 1)]
+                members_of += [ends[step, field]]
+                for pair, (i, j) in enumerate(index):
+                    product = members_of[i] * members_of[j]
+                    for r in range(0, depth_z, 8):
+                        totals[pair] = totals[pair] + product[r : r + 8]
         return tuple(totals)
 
     zeros = tuple(jnp.zeros((8, lanes), jnp.float32) for pair in index)
-    sums = lax.fori_loop(0, rows, last_apply, zeros)
+    sums = lax.fori_loop(0, rows // 4, last_apply, zeros)
     square = jnp.concatenate(
         [jnp.sum(total, axis=0, keepdims=True) for total in sums]
         + [jnp.zeros((16 - len(index), lanes), jnp.float32)],
@@ -757,7 +770,7 @@
                 pltpu.SemaphoreType.DMA((members,)),
             ],
             compiler_params=pltpu.CompilerParams(
-                collective_id=0, has_side_effects=True, vmem_limit_bytes=48 * 1024 * 1024
+                collective_id=0, has_side_effects=True, vmem_limit_bytes=63 * 1024 * 1024
             ),
         )(
             previous.reshape(flat),

time: 48.4 us -> 41.7 us (0.86)
  Pallas kernels: 43.8 us -> 39.9 us
  local copies, waits for them, and re-layouts: 4.37 us -> 1.67 us
    pallas_call x1, Pallas kernels: 43.8 us -> 39.9 us  [body(): pl.pallas_call(functools.partial(kernel, sx_count, sy_count, tables), out...]
    unnamed x9 -> x1, local copies, waits for them, and re-layouts: 4.37 us -> 1.67 us
where the time goes in v4:
time: 41.7 us; the launch traced here: 41.6 us
  Pallas kernels  39.9 us (96%)
  local copies, waits for them, and re-layouts  1.67 us (4%)
    pallas_call x1, Pallas kernels, body(): pl.pallas_call(functools.partial(kernel, sx_count, sy_count, tables), out...  39.9 us
    unnamed x1, local copies, waits for them, and re-layouts  1.67 us

profile of v4, /device:TPU:0, one launch (start us, length us, event | category | flops | bytes accessed | tf_op | source)
XLA Modules:
  0.0 41.6 jit_solution(11590903808952625209)
XLA Ops:
  0.0 39.9 %shard_map.46 = f32[2,256,128]{2,1,0:T(8,128)} custom-call(f32[256,128]{1,0:T(8,128)} %bitcast.7, f32[2,256,128]{2,1,0:T(8,128)} %bitcast.6, f32[256,128]{1,0:T(8,128)} %bitcast.8, f32[256,128]{1,0:T(8,128)} %bitcast.9), custom_call_target="tpu_custom_call" | custom-call | tf_op jit(solution)/shard_map/pallas_call | solution.py:735
  39.9 1.7 %copy.6 = f32[2,16,16,128]{3,2,1,0:T(8,128)} copy(f32[2,16,16,128]{3,2,1,0:T(8,128)} %bitcast.5) | data formatting | bytes 524288

commit v5 on v4

--- a/solution.py
+++ b/solution.py
@@ -196,6 +196,13 @@
         other = lax.rem(me + offset, members)
         return {"sx": other // sy_count, "sy": lax.rem(other, sy_count)}
 
+    def greet(offset, carry):
+        pl.semaphore_signal(barrier, inc=1, device_id=member_at(offset), device_id_type=MESH)
+        return carry
+
+    lax.fori_loop(1, members, greet, 0)
+    pl.semaphore_signal(barrier, inc=1, device_id={"section": 1 - half}, device_id_type=MESH)
+
     loads = [
         pltpu.make_async_copy(source, target, load_sem.at[at])
         for at, (source, target) in enumerate((
@@ -204,20 +211,28 @@
     ]
     for one in loads:
         one.start()
-    ext_a[...] = jnp.zeros_like(ext_a)
-    ext_b[...] = jnp.zeros_like(ext_b)
-    got_a[...] = jnp.zeros_like(got_a)
-    got_b[...] = jnp.zeros_like(got_b)
-    got_c[...] = jnp.zeros_like(got_c)
-    for field in range(2):
-        hist[0][field] = jnp.zeros(hist[0].shape[1:], jnp.float32)
-
-    def greet(offset, carry):
-        pl.semaphore_signal(barrier, inc=1, device_id=member_at(offset), device_id_type=MESH)
-        return carry
-
-    lax.fori_loop(1, members, greet, 0)
-    pl.semaphore_signal(barrier, inc=1, device_id={"section": 1 - half}, device_id_type=MESH)
+
+    wide = rows + 2 * DEPTH
+    left, right = lax.rem(sx + sx_count - 1, sx_count), lax.rem(sx + 1, sx_count)
+    below, above = lax.rem(sy + sy_count - 1, sy_count), lax.rem(sy + 1, sy_count)
+    has_left, has_right = sx > 0, sx < sx_count - 1
+    has_below, has_above = sy > 0, sy < sy_count - 1
+
+    def clear(missing, *views):
+        def run():
+            for view in views:
+                view[...] = jnp.zeros(view.shape, jnp.float32)
+
+        pl.when(jnp.logical_not(missing))(run)
+
+    clear(has_left, ext_a.at[:, DEPTH - 1, :, 0:lanes], ext_b.at[:, 0:DEPTH, :, 0:lanes],
+          hist[0].at[:, 0:DEPTH, :, 0:lanes])
+    clear(has_right, ext_a.at[:, top, :, 0:lanes], ext_b.at[:, top:wide, :, 0:lanes],
+          hist[0].at[:, top:wide, :, 0:lanes])
+    for side, there in ((0, has_above), (1, has_below)):
+        clear(there, got_a.at[side], got_b.at[side, 1], got_c.at[side, 1])
+        clear(there & has_left, got_b.at[side, 0], got_c.at[side, 0])
+        clear(there & has_right, got_b.at[side, 2], got_c.at[side, 2])
 
     lane_group = lax.broadcasted_iota(jnp.int32, (depth_z, lanes), 1) // DEPTH
 
@@ -256,9 +271,6 @@
     def column(ref, x):
         return ref[pl.ds(x, depth_z, stride=rows), :]
 
-    for one in loads:
-        one.wait()
-
     def planes(fn, least, most, batch):
         def several(first, count):
             stores = [fn(first + step) for step in range(count)]
@@ -277,27 +289,34 @@
         if left_over:
             several(most - left_over, left_over)
 
-    def own_coefs(x):
-        before, diffusivity = column(prev_ref, x), column(diff_ref, x)
+    def section_coefs(x):
+        diffusivity = column(diff_ref, x)
         cells = [column(sec_ref.at[j], x) for j in range(2)]
         coefs = [diffusivity * (1.0 + 0.5 * jnp.tanh(cells[j])) for j in range(2)]
-        coef = diffusivity * (1.0 + 0.5 * jnp.tanh(before))
-        slope = column(react_ref, x) * (1.0 - 3.0 * before * before)
 
         def store():
             for j in range(2):
                 ext_a[j, x + DEPTH, :, 0:lanes] = cells[j]
                 ext_a[2 + j, x + DEPTH, :, 0:lanes] = coefs[j]
+
+        return store
+
+    def frozen_coefs(x):
+        before = column(prev_ref, x)
+        coef = column(diff_ref, x) * (1.0 + 0.5 * jnp.tanh(before))
+        slope = column(react_ref, x) * (1.0 - 3.0 * before * before)
+
+        def store():
             ext_b[0, x + DEPTH, :, 0:lanes] = coef
             ext_b[1, x + DEPTH, :, 0:lanes] = slope
 
         return store
 
-    planes(own_coefs, 0, rows, 4)
+    for one in loads[:2]:
+        one.wait()
+    planes(section_coefs, 0, rows, 4)
     for j in range(4):
         pack(lambda x: ext_a[j, x + DEPTH, :, 0:lanes], pack_a.at[0, j], pack_a.at[1, j])
-    for j in range(2):
-        pack(lambda x: ext_b[j, x + DEPTH, :, 0:lanes], pack_b.at[0, j], pack_b.at[1, j])
 
     pl.semaphore_wait(barrier, members)
 
@@ -315,11 +334,6 @@
             device_id_type=MESH,
         )
 
-    wide = rows + 2 * DEPTH
-    left, right = lax.rem(sx + sx_count - 1, sx_count), lax.rem(sx + 1, sx_count)
-    below, above = lax.rem(sy + sy_count - 1, sy_count), lax.rem(sy + 1, sy_count)
-    has_left, has_right = sx > 0, sx < sx_count - 1
-    has_below, has_above = sy > 0, sy < sy_count - 1
     own = pl.ds(0, lanes)
     low_rows, high_rows = pl.ds(0, DEPTH), pl.ds(top, DEPTH)
 
@@ -391,6 +405,11 @@
         ),
     ))
     start(copies_a)
+    for one in loads[2:]:
+        one.wait()
+    planes(frozen_coefs, 0, rows, 4)
+    for j in range(2):
+        pack(lambda x: ext_b[j, x + DEPTH, :, 0:lanes], pack_b.at[0, j], pack_b.at[1, j])
     copies_b = strips(pack_b, got_b, True)
     copies_b += slabs(
         ext_b.at[:, pl.ds(DEPTH, DEPTH), :, own],
@@ -529,18 +548,18 @@
 
         return store
 
-    copies_c = slabs(
-        hist[0].at[:, pl.ds(DEPTH, DEPTH), :, own],
-        hist[0].at[:, pl.ds(top - DEPTH, DEPTH), :, own],
-        lambda where: hist[0].at[:, where, :, own],
-    )
+    copies_c = []
     for at in range(4):
         swap[at].wait_recv()
         planes(first_scaled, at * chunk, (at + 1) * chunk, chunk)
-        if (at + 1) * chunk == DEPTH:
-            start(copies_c[0:1])
-        if (at + 1) * chunk == rows:
-            start(copies_c[1:2])
+        low = (at + 1) * chunk <= DEPTH
+        one = copy(
+            hist[0].at[:, pl.ds(DEPTH + at * chunk, chunk), :, own],
+            hist[0].at[:, pl.ds(at * chunk + (top if low else DEPTH - rows), chunk), :, own],
+            {"sx": left if low else right},
+        )
+        copies_c.append((has_left, has_right, one) if low else (has_right, has_left, one))
+        start(copies_c[-1:])
     for j in range(2):
         pack(lambda x: hist[0][j, x + DEPTH, :, 0:lanes], pack_c.at[0, j], pack_c.at[1, j])
     more_c = strips(pack_c, got_c, True)
@@ -764,8 +783,8 @@
                 vmem((2, 3, 2, depth_z, lanes), f32),
                 vmem((members, 1, lanes), f32),
                 pltpu.SemaphoreType.DMA((4,)),
-                pltpu.SemaphoreType.DMA((32,)),
-                pltpu.SemaphoreType.DMA((32,)),
+                pltpu.SemaphoreType.DMA((40,)),
+                pltpu.SemaphoreType.DMA((40,)),
                 pltpu.SemaphoreType.DMA((members,)),
                 pltpu.SemaphoreType.DMA((members,)),
             ],

time: 41.7 us -> 40.7 us (0.976)
  Pallas kernels: 39.9 us -> 38.8 us
    pallas_call x1, Pallas kernels: 39.9 us -> 38.8 us  [body(): pl.pallas_call(functools.partial(kernel, sx_count, sy_count, tables), out...]
where the time goes in v5:
time: 40.7 us; the launch traced here: 40.5 us
  Pallas kernels  38.8 us (95%)
  local copies, waits for them, and re-layouts  1.67 us (4%)
    pallas_call x1, Pallas kernels, body(): pl.pallas_call(functools.partial(kernel, sx_count, sy_count, tables), out...  38.8 us
    unnamed x1, local copies, waits for them, and re-layouts  1.67 us

profile of v5, /device:TPU:0, one launch (start us, length us, event | category | flops | bytes accessed | tf_op | source)
XLA Modules:
  0.0 40.5 jit_solution(2741281745906168670)
XLA Ops:
  0.0 38.8 %shard_map.46 = f32[2,256,128]{2,1,0:T(8,128)} custom-call(f32[256,128]{1,0:T(8,128)} %bitcast.7, f32[2,256,128]{2,1,0:T(8,128)} %bitcast.6, f32[256,128]{1,0:T(8,128)} %bitcast.8, f32[256,128]{1,0:T(8,128)} %bitcast.9), custom_call_target="tpu_custom_call" | custom-call | tf_op jit(solution)/shard_map/pallas_call | solution.py:754
  38.8 1.7 %copy.6 = f32[2,16,16,128]{3,2,1,0:T(8,128)} copy(f32[2,16,16,128]{3,2,1,0:T(8,128)} %bitcast.5) | data formatting | bytes 524288

commit v6 on v5

--- a/solution.py
+++ b/solution.py
@@ -420,12 +420,6 @@
 
     receive(copies_a)
 
-    for j in range(4):
-        def put_a(x, plane):
-            ext_a[j, x + DEPTH, :, lanes : 2 * lanes] = plane
-
-        unpack(got_a[0, j], got_a[1, j], range(rows), put_a)
-
     q_own = [[pick(q_table[m][j], q_table[2 + m][2 + j]) for j in range(2)] for m in range(2)]
     q_far = [[pick(q_table[2 + m][j], q_table[m][2 + j]) for j in range(2)] for m in range(2)]
     c_own = [[pick(c_table[m][j], c_table[2 + m][2 + j]) for j in range(2)] for m in range(2)]
@@ -479,6 +473,11 @@
     chunk = rows // 4
     swap = []
     for at in range(4):
+        for j in range(4):
+            def put_a(x, plane):
+                ext_a[j, x + DEPTH, :, lanes : 2 * lanes] = plane
+
+            unpack(got_a[0, j], got_a[1, j], range(at * chunk, (at + 1) * chunk), put_a)
         planes(fluxes, at * chunk, (at + 1) * chunk, chunk)
         piece = pl.ds(at * chunk, chunk)
         one = copy(part_out.at[:, piece], part_in.at[:, piece], {"section": 1 - half})
@@ -789,13 +788,18 @@
                 pltpu.SemaphoreType.DMA((members,)),
             ],
             compiler_params=pltpu.CompilerParams(
-                collective_id=0, has_side_effects=True, vmem_limit_bytes=63 * 1024 * 1024
+                collective_id=0, has_side_effects=True, vmem_limit_bytes=48 * 1024 * 1024
             ),
         )(
-            previous.reshape(flat),
-            sections.reshape((2,) + flat),
-            diffusivity.reshape(flat),
-            reaction.reshape(flat),
+            *(
+                pltpu.with_memory_space_constraint(cells, pltpu.HBM)
+                for cells in (
+                    previous.reshape(flat),
+                    sections.reshape((2,) + flat),
+                    diffusivity.reshape(flat),
+                    reaction.reshape(flat),
+                )
+            )
         ).reshape(sections.shape)
 
     in_specs = (

time: 40.7 us -> 38.9 us (0.956)
  local copies, waits for them, and re-layouts: 1.67 us -> 0.71 us
  Pallas kernels: 38.8 us -> 38 us
    unnamed x1, local copies, waits for them, and re-layouts: 1.67 us -> 0.71 us
    pallas_call x1, Pallas kernels: 38.8 us -> 38 us  [body(): pl.pallas_call(functools.partial(kernel, sx_count, sy_count, tables), out...]
where the time goes in v6:
time: 38.9 us; the launch traced here: 38.7 us
  Pallas kernels  38 us (98%)
  local copies, waits for them, and re-layouts  0.71 us (2%)
    pallas_call x1, Pallas kernels, body(): pl.pallas_call(functools.partial(kernel, sx_count, sy_count, tables), out...  38 us

profile of v6, /device:TPU:0, one launch (start us, length us, event | category | flops | bytes accessed | tf_op | source)
XLA Modules:
  0.0 38.7 jit_solution(13276326020897100491)
XLA Ops:
  0.0 38.0 %shard_map.46 = f32[2,256,128]{2,1,0:T(8,128)S(1)} custom-call(f32[256,128]{1,0:T(8,128)} %bitcast.7, f32[2,256,128]{2,1,0:T(8,128)} %bitcast.6, f32[256,128]{1,0:T(8,128)} %bitcast.8, f32[256,128]{1,0:T(8,128)} %bitcast.9), custom_call_target="tpu_custom_call" | custom-call | tf_op jit(solution)/shard_map/pallas_call | solution.py:753
  38.0 0.7 %copy.6 = f32[2,16,16,128]{3,2,1,0:T(8,128)} copy(f32[2,16,16,128]{3,2,1,0:T(8,128)S(1)} %bitcast.5) | data formatting | bytes 524288

commit v7 on v6

--- a/solution.py
+++ b/solution.py
@@ -588,7 +588,7 @@
 
             return store
 
-        planes(apply, m + 1, wide - 1 - m, 4)
+        planes(apply, m + 1, wide - 1 - m, 6)
 
     index = [(i, j) for i in range(ITERS + 1) for j in range(i, ITERS + 1)]
 

time: 38.9 us -> 37.8 us (0.972)
  Pallas kernels: 38 us -> 37 us
    pallas_call x1, Pallas kernels: 38 us -> 37 us  [body(): pl.pallas_call(functools.partial(kernel, sx_count, sy_count, tables), out...]
where the time goes in v7:
time: 37.8 us; the launch traced here: 37.7 us
  Pallas kernels  37 us (98%)
  local copies, waits for them, and re-layouts  0.71 us (2%)
    pallas_call x1, Pallas kernels, body(): pl.pallas_call(functools.partial(kernel, sx_count, sy_count, tables), out...  37 us

profile of v7, /device:TPU:0, one launch (start us, length us, event | category | flops | bytes accessed | tf_op | source)
XLA Modules:
  0.0 37.7 jit_solution(11689332169753826318)
XLA Ops:
  0.0 37.0 %shard_map.46 = f32[2,256,128]{2,1,0:T(8,128)S(1)} custom-call(f32[256,128]{1,0:T(8,128)} %bitcast.7, f32[2,256,128]{2,1,0:T(8,128)} %bitcast.6, f32[256,128]{1,0:T(8,128)} %bitcast.8, f32[256,128]{1,0:T(8,128)} %bitcast.9), custom_call_target="tpu_custom_call" | custom-call | tf_op jit(solution)/shard_map/pallas_call | solution.py:753
  37.0 0.7 %copy.6 = f32[2,16,16,128]{3,2,1,0:T(8,128)} copy(f32[2,16,16,128]{3,2,1,0:T(8,128)S(1)} %bitcast.5) | data formatting | bytes 524288
